TPU v7x, 512 devices: a whole 4x4x16 slice. The times are simulated.
512 devices in a mesh: pipe: 16 (over y, x), expert: 32 (over z, core).
Axes of the slice: x: 4, y: 4, z: 16, core: 2. Of those that a mesh axis runs over, the one named last changes fastest.
Arguments:
- token_rows: bfloat16 [8192, 7168], P('expert', 'pipe'), may hold values from -6 to 6
- row_scale: bfloat16 [8192], P('expert'), may hold values from 0.25 to 4
- routes: int32 [8192, 8], P('expert'), may hold values from 0 to 255, as said below
- gate_weights: bfloat16 [8192, 8], P('expert'), may hold values from 0.049804688 to 0.59765625
- up_weight: bfloat16 [32, 7168, 2048], P('expert', 'pipe'), may hold values from -0.0625 to 0.0625
- down_weight: bfloat16 [32, 2048, 7168], P('expert', None, 'pipe'), may hold values from -0.125 to 0.125
Outputs:
- combined: float32 [8192, 7168], P('expert', 'pipe')
Inputs may be any that keep to these rules, and one draw needn't show every extreme that they name: `routes`: A token names 8 different experts. Among the 256 tokens of one index of expert, no expert below 32 is named by more than 16 of them, and in every draw one expert below 32 is named by exactly 16 tokens of every index of expert.
All inputs are finite; a program needn't handle non-finite values.
Results may differ from a plain program's by a relative error of at most 0.004.
Values may be sent and summed in bfloat16 or wider, within the bound.
No kernel may reach another device: no remote copies, remote signals or barrier semaphores. Data moves between devices by JAX's collectives and lax.ppermute only.
A program may use at most 64 MiB of HBM per device.

v0:
```python
import jax
import jax.numpy as jnp
from jax import lax
from jax.sharding import PartitionSpec as P


def on_device(token_rows, row_scale, routes, gate_weights, up_weight, down_weight):
    expert_count = lax.axis_size("expert")
    tokens_here = token_rows.shape[0]
    width_part = token_rows.shape[1]
    top_routes = routes.shape[1]
    capacity = tokens_here // 16
    slot_total = expert_count * capacity
    entries = tokens_here * top_routes
    flat_expert = routes.reshape(entries)
    expert_hot = (
        flat_expert[:, None] == jnp.arange(expert_count, dtype=jnp.int32)[None, :]
    ).astype(jnp.int32)
    earlier = jnp.cumsum(expert_hot, axis=0) - expert_hot
    slot_rank = jnp.sum(earlier * expert_hot, axis=1)
    in_window = flat_expert < expert_count
    position = jnp.where(in_window, flat_expert * capacity + slot_rank, slot_total)
    entry_token = jnp.arange(entries, dtype=jnp.int32) // top_routes
    slot_token = (
        jnp.full((slot_total,), tokens_here, jnp.int32).at[position].set(entry_token, mode="drop")
    )
    padded_rows = jnp.concatenate([token_rows, jnp.zeros((1, width_part), jnp.bfloat16)], axis=0)
    padded_scale = jnp.concatenate([row_scale, jnp.zeros((1,), jnp.bfloat16)], axis=0)
    send_rows = padded_rows[slot_token].reshape(expert_count, capacity, width_part)
    send_scale = padded_scale[slot_token].reshape(expert_count, capacity)
    got_rows, got_scale = (
        lax.all_to_all(send_rows, "expert", split_axis=0, concat_axis=0, tiled=True),
        lax.all_to_all(send_scale, "expert", split_axis=0, concat_axis=0, tiled=True),
    )
    flat_rows = got_rows.reshape(slot_total, width_part)
    flat_scale = got_scale.reshape(slot_total).astype(jnp.float32)
    up_local = up_weight[0]
    down_local = down_weight[0]
    first_contract = (((0,), (1,)), ((), ()))
    second_contract = (((0,), (0,)), ((), ()))
    partial_term = lax.dot_general(
        up_local, flat_rows, first_contract, preferred_element_type=jnp.float32
    )
    preact = lax.psum(partial_term, "pipe")
    active = jax.nn.silu(preact * flat_scale[None, :]).astype(jnp.bfloat16)
    out_rows = lax.dot_general(
        active, down_local, second_contract, preferred_element_type=jnp.float32
    )
    expert_out = out_rows.astype(jnp.bfloat16).reshape(expert_count, capacity, width_part)
    returned = lax.all_to_all(expert_out, "expert", split_axis=0, concat_axis=0, tiled=True)
    flat_back = returned.reshape(slot_total, width_part)
    gate_flat = gate_weights.reshape(entries)
    combine_matrix = (
        jnp.zeros((tokens_here, slot_total), jnp.bfloat16)
        .at[entry_token, position]
        .set(gate_flat, mode="drop")
    )
    return jnp.dot(combine_matrix, flat_back, preferred_element_type=jnp.float32)


def solution(mesh):
    return jax.shard_map(
        on_device,
        mesh=mesh,
        in_specs=(
            P("expert", "pipe"),
            P("expert"),
            P("expert", None),
            P("expert", None),
            P("expert", "pipe", None),
            P("expert", None, "pipe"),
        ),
        out_specs=P("expert", "pipe"),
        check_vma=False,
    )
```

profile of v0, /device:TPU:6, one launch (start us, length us, event | category | flops | bytes accessed | tf_op | source)
XLA Modules:
  0.0 268.6 jit_solution(11065865325417823729)
XLA Ops:
  6.5 0.0 copy-start
  6.5 0.0 all-reduce.3.cloned.1.call-start
  6.5 0.8 broadcast_compare_fusion
  7.4 0.7 broadcast_multiply_fusion
  8.1 0.8 copy.19
  8.9 0.1 eq.29
  9.0 0.1 eq.25
  9.1 0.2 copy.17
  9.3 0.1 lt.44
  9.4 0.1 copy.18
  9.6 0.1 mul.33
  9.7 9.1 %reduce-window.6 = s32[32,16,128]{2,1,0:T(8,128)S(1)} reduce-window(s32[32,16,128]{2,1,0:T(8,128)S(1)} %fusion.9, s32[]{:T(128)} %constant.37.clone.1), window={size=1x1x128 pad=0_0x0_0x127_0}, to_apply=%region_0.0 | reduce-window | flops 8323072 | bytes 524292 | tf_op jit(solution)/shard_map/reduce-window
  18.8 0.1 slice.12
  18.9 0.2 copy.27
  19.2 0.2 reduce-window.9
  19.4 0.1 broadcast_add_fusion
  19.5 0.1 fusion.8
  19.7 8.0 %scatter_custom_fusion = s32[512]{0:T(512)S(1)} fusion(s32[2048]{0:T(1024)S(1)} %bitcast.45, s32[2048]{0:T(1024)S(1)} %add_select_fusion, s32[]{:T(128)} %constant.40.clone.1), kind=kCustom, calls=%fused_computation.43 | custom fusion | bytes 2052 | tf_op jit(solution)/shard_map/scatter | solution.py:25
  27.7 1.1 copy.24
  28.8 2.0 gather_fusion
  30.8 49.0 %all_to_all.20 = bf16[32,16,448]{2,1,0:T(8,128)(2,1)S(1)} all-to-all(bf16[32,16,448]{2,1,0:T(8,128)(2,1)S(1)} %bitcast.41), channel_id=1, replica_groups=mesh['pipe'=16,'expert'=32] {'expert'}, dimensions={0} | all-to-all | bytes 917504 | tf_op jit(solution)/shard_map/all_to_all | solution.py:32
  79.9 0.0 copy-done
  79.9 0.0 copy-start.4
  79.9 3.2 %convolution_bitcast_fusion = f32[2048,512]{0,1:T(8,128)} fusion(bf16[512,448]{1,0:T(8,128)(2,1)S(1)} %bitcast.42, bf16[1,448,2048]{2,1,0:T(8,128)(2,1)S(1)} %copy-done), kind=kOutput, calls=%fused_computation.5 | convolution fusion | flops 939524096 | bytes 6488064 | tf_op jit(solution)/shard_map/dot_general | solution.py:41
  83.1 0.0 all-reduce.3.cloned.1.call-update
  83.1 0.0 copy-done.4
  83.2 3.5 %gather_fusion.1 = bf16[512]{0:T(512)(128)(2,1)S(1)} fusion(bf16[257]{0:T(512)(128)(2,1)S(1)} %pad_maximum_fusion, s32[1024]{0:T(1024)S(1)} %pad_clamp_fusion), kind=kCustom, calls=%fused_computation.1 | custom fusion | bytes 4096 | tf_op jit(solution)/shard_map/gather | solution.py:30
  86.7 0.1 all_to_all.16
  86.8 15.4 %all_to_all.21 = bf16[32,1,16]{2,1,0:T(2,128)(2,1)S(1)} all-to-all(bf16[32,1,16]{2,1,0:T(2,128)(2,1)S(1)} %all_to_all.16), channel_id=1, replica_groups=mesh['pipe'=16,'expert'=32] {'expert'}, dimensions={0} | all-to-all | bytes 2048 | tf_op jit(solution)/shard_map/all_to_all | solution.py:33
  102.2 0.1 convert_reduce_fusion
  102.2 0.1 reshape.141
  102.3 0.0 copy-start.1
  102.3 0.0 copy-start.2
  102.3 106.7 %all-reduce.3.cloned.1.call-done = f32[2048,512]{0,1:T(8,128)} async-done(((f32[2048,512]{0,1:T(8,128)}), f32[2048,512]{0,1:T(8,128)}) %all-reduce.3.cloned.1.call-update) | async-done | bytes 4194320 | tf_op jit(solution)/shard_map/psum | solution.py:44
  209.0 4.3 %fusion.3 = bf16[512,448]{0,1:T(8,128)(2,1)S(1)} fusion(bf16[1,2048,448]{1,2,0:T(8,128)(2,1)} %param.11, f32[2048,512]{0,1:T(8,128)} %all-reduce.3.cloned.1.call-done, f32[512]{0:T(512)S(1)} %reshape.141), kind=kOutput, calls=%fused_computation.9 | convolution fusion | flops 946044928 | bytes 6490112 | tf_op jit(solution)/shard_map/dot_general | solution.py:46
  213.4 1.0 copy.26
  214.4 12.6 %all-to-all-start.2 = ((bf16[32,16,448]{2,1,0:T(8,128)(2,1)}), bf16[32,16,448]{2,1,0:T(8,128)(2,1)S(1)}, u32[]{:S(2)}, u32[]{:S(2)}) async-start(bf16[32,16,448]{2,1,0:T(8,128)(2,1)} %bitcast.10), calls=%async_computation.2 | async-start | bytes 1048576 | tf_op jit(solution)/shard_map/all_to_all | solution.py:50
  226.9 0.0 copy-done.1
  227.0 0.1 copy.23
  227.1 0.1 reshape.168
  227.2 0.0 copy-done.3
  227.2 0.1 multiply_reduce_fusion
  227.3 0.0 copy-done.2
  227.3 0.1 and_reduce_fusion
  227.4 14.7 %scatter_custom_fusion.1 = bf16[131072]{0:T(1024)(128)(2,1)S(1)} fusion(s32[2048]{0:T(1024)S(1)} %broadcast_select_fusion, bf16[2048]{0:T(1024)(128)(2,1)S(1)} %reshape.168, bf16[]{:T(256)} %constant.17.clone.1), kind=kCustom, calls=%fused_computation.17 | custom fusion | bytes 262146
  242.1 0.2 reshape.140
  242.3 18.4 %all-to-all-done.2 = bf16[32,16,448]{2,1,0:T(8,128)(2,1)S(1)} async-done(((bf16[32,16,448]{2,1,0:T(8,128)(2,1)}), bf16[32,16,448]{2,1,0:T(8,128)(2,1)S(1)}, u32[]{:S(2)}, u32[]{:S(2)}) %all-to-all-start.2) | async-done | bytes 458784 | tf_op jit(solution)/shard_map/all_to_all | solution.py:50
  260.7 1.1 fusion.18
  (9 shorter events, 0.1 us)
Async XLA Ops:
  6.5 73.3 %copy-start = (bf16[1,448,2048]{2,1,0:T(8,128)(2,1)S(1)}, bf16[1,448,2048]{2,1,0:T(8,128)(2,1)}, u32[]{:S(2)}) copy-start(bf16[1,448,2048]{2,1,0:T(8,128)(2,1)} %param.10) | copy-start | bytes 5505028
  6.5 202.5 %all-reduce.3.cloned.1.call-start = ((), (), s32[]{:S(2)}) async-start(), calls=%async_computation.3 | async-start | bytes 8388608 | tf_op jit(solution)/shard_map/psum | solution.py:44
  79.9 3.3 %copy-start.4 = (bf16[256]{0:T(256)(128)(2,1)S(1)}, bf16[256]{0:T(256)(128)(2,1)}, u32[]{:S(2)}) copy-start(bf16[256]{0:T(256)(128)(2,1)} %param.7) | copy-start | bytes 1540
  102.3 124.7 %copy-start.1 = (bf16[256,8]{0,1:T(8,128)(2,1)S(1)}, bf16[256,8]{0,1:T(8,128)(2,1)}, u32[]{:S(2)}) copy-start(bf16[256,8]{0,1:T(8,128)(2,1)} %param.9) | copy-start | bytes 12292
  102.3 124.9 %copy-start.3 = (s32[2]{0:T(128)S(1)}, s32[2]{0:T(128)}, u32[]{:S(2)}) copy-start(s32[2]{0:T(128)} %constant.51) | copy-start | bytes 28
  102.3 125.0 %copy-start.2 = (s32[2]{0:T(128)S(1)}, s32[2]{0:T(128)}, u32[]{:S(2)}) copy-start(s32[2]{0:T(128)} %constant.54) | copy-start | bytes 28
  214.4 46.3 %all-to-all-start.2 = ((bf16[32,16,448]{2,1,0:T(8,128)(2,1)}), bf16[32,16,448]{2,1,0:T(8,128)(2,1)S(1)}, u32[]{:S(2)}, u32[]{:S(2)}) async-start(bf16[32,16,448]{2,1,0:T(8,128)(2,1)} %bitcast.10), calls=%async_computation.2 | async-start | bytes 1048576 | tf_op jit(solution)/shard_map/all_to_all | solution.py:50
Sparse Core Ops, SparseCore 0:
  83.3 125.7 all-reduce.2
where the time goes:
time: 270 us; the launch traced here: 269 us
  waiting for transfers between devices  125 us (46%)
  blocking collectives  64.4 us (24%)
  local copies, waits for them, and re-layouts  32.9 us (12%)
  between operations  13.6 us (5%)
  starting transfers between devices  12.6 us (5%)
  other arithmetic  11.4 us (4%)
  matrix products  8.68 us (3%)
    psum x1, waiting for transfers between devices, on_device(): preact = lax.psum(partial_term, 'pipe')  107 us
    all_to_all x1, blocking collectives, on_device(): lax.all_to_all(send_rows, 'expert', split_axis=0, concat_axis=0, tiled=True)  49 us
    all_to_all x1, waiting for transfers between devices, on_device(): lax.all_to_all(expert_out, 'expert', split_axis=0, concat_axis=0, tiled=T...  18.4 us
    unnamed x14, local copies, waits for them, and re-layouts  16.7 us
    all_to_all x1, blocking collectives, on_device(): lax.all_to_all(send_scale, 'expert', split_axis=0, concat_axis=0, tiled=T...  15.4 us
    all_to_all x1, starting transfers between devices, on_device(): lax.all_to_all(expert_out, 'expert', split_axis=0, concat_axis=0, tiled=T...  12.6 us
    another operation x3, other arithmetic  9.41 us
    scatter x1, local copies, waits for them, and re-layouts, on_device(): jnp.full((slot_total,), tokens_here, jnp.int32).at[position]  8.04 us
  transfers between devices with their start and end apart: 2, of which 2 were waited for; matrix products, arithmetic and copies ran while one was open for 7% of the time, Pallas kernels for 0%

commit v1 on v0

v1 whole, which is shorter than its diff:
```python
import functools

import jax
import jax.numpy as jnp
from jax import lax
from jax.experimental import pallas as pl
from jax.experimental.pallas import tpu as pltpu
from jax.sharding import PartitionSpec as P

F32 = jnp.float32
BF16 = jnp.bfloat16
WIRE = jnp.float16
WIRE_GAIN = 64.0
NT = (((1,), (1,)), ((), ()))
NN = (((1,), (0,)), ((), ()))
TN = (((0,), (0,)), ((), ()))
VMEM_LIMIT = 40 * 1024 * 1024


def vmem_spec():
    return pl.BlockSpec(memory_space=pltpu.VMEM)


def slot_hits(routes_t, experts, capacity):
    tokens = routes_t.shape[1]
    slots = experts * capacity
    expert_id = lax.broadcasted_iota(jnp.int32, (experts, tokens), 0)
    hot = jnp.zeros((experts, tokens), jnp.bool_)
    for k in range(routes_t.shape[0]):
        hot = hot | (routes_t[k : k + 1, :] == expert_id)
    hot_f = jnp.where(hot, 1.0, 0.0)
    before = lax.broadcasted_iota(jnp.int32, (tokens, tokens), 0) < lax.broadcasted_iota(
        jnp.int32, (tokens, tokens), 1
    )
    rank = lax.dot_general(
        hot_f.astype(BF16),
        jnp.where(before, 1.0, 0.0).astype(BF16),
        NN,
        preferred_element_type=F32,
    )
    rank = jnp.where(hot, rank, -1.0)
    rank_slots = jnp.broadcast_to(rank[:, None, :], (experts, capacity, tokens)).reshape(
        slots, tokens
    )
    place = (lax.broadcasted_iota(jnp.int32, (slots, tokens), 0) % capacity).astype(F32)
    return rank_slots == place


def pick_kernel(experts, capacity, rows_ref, scale_ref, routes_ref, out_ref):
    width = rows_ref.shape[0]
    hits = jnp.where(slot_hits(routes_ref[...], experts, capacity), 1.0, 0.0)
    picked = lax.dot_general(hits.astype(BF16), rows_ref[...], NT, preferred_element_type=F32)
    scale = jnp.sum(hits * scale_ref[...].astype(F32), axis=1, keepdims=True)
    out_ref[:, :width] = picked.astype(BF16)
    out_ref[:, width:] = jnp.broadcast_to(
        scale.astype(BF16), (out_ref.shape[0], out_ref.shape[1] - width)
    )


def gate_kernel(experts, capacity, routes_ref, gate_ref, out_ref):
    routes_t = routes_ref[...]
    tokens = routes_t.shape[1]
    expert_id = lax.broadcasted_iota(jnp.int32, (experts, tokens), 0)
    gate = jnp.zeros((experts, tokens), F32)
    for k in range(routes_t.shape[0]):
        gate = jnp.where(
            routes_t[k : k + 1, :] == expert_id, gate_ref[k : k + 1, :].astype(F32), gate
        )
    gate_slots = jnp.broadcast_to(gate[:, None, :], (experts, capacity, tokens)).reshape(
        experts * capacity, tokens
    )
    hits = slot_hits(routes_t, experts, capacity)
    out_ref[...] = jnp.where(hits, gate_slots, 0.0).astype(BF16)


def down_kernel(active_ref, down_ref, out_ref):
    out_ref[...] = lax.dot_general(
        active_ref[...], down_ref[...], NT, preferred_element_type=F32
    ).astype(BF16)


def combine_kernel(back_ref, gate_ref, out_ref):
    out_ref[...] = lax.dot_general(
        back_ref[...], gate_ref[...], TN, preferred_element_type=F32
    )


def on_device(token_rows, row_scale, routes, gate_weights, up_weight, down_weight):
    experts = lax.axis_size("expert")
    shares = lax.axis_size("pipe")
    tokens, width = token_rows.shape
    hidden = up_weight.shape[2]
    capacity = tokens // 16
    slots = experts * capacity
    share_slots = slots // shares
    padded = -(-(width + 1) // 128) * 128
    params = pltpu.CompilerParams(vmem_limit_bytes=VMEM_LIMIT)
    rows_t = token_rows.T
    routes_t = routes.T
    gate_t = gate_weights.T
    scale_row = row_scale.reshape(1, tokens)

    send = pl.pallas_call(
        functools.partial(pick_kernel, experts, capacity),
        out_shape=jax.ShapeDtypeStruct((slots, padded), BF16),
        in_specs=[vmem_spec()] * 3,
        out_specs=vmem_spec(),
        compiler_params=params,
        name="pick",
    )(rows_t, scale_row, routes_t)
    got = lax.all_to_all(
        send.reshape(experts, capacity, padded), "expert", 0, 0, tiled=True
    ).reshape(slots, padded)
    gate_slots = pl.pallas_call(
        functools.partial(gate_kernel, experts, capacity),
        out_shape=jax.ShapeDtypeStruct((slots, tokens), BF16),
        in_specs=[vmem_spec()] * 2,
        out_specs=vmem_spec(),
        compiler_params=params,
        name="gates",
    )(routes_t, gate_t)

    terms = jnp.dot(got[:, :width], up_weight[0], preferred_element_type=F32)
    terms = (terms * WIRE_GAIN).astype(WIRE)
    parts = lax.all_to_all(
        terms.reshape(shares, share_slots, hidden), "pipe", 0, 0, tiled=True
    )
    share = lax.axis_index("pipe")
    mine = lax.dynamic_slice(got, (share * share_slots, width), (share_slots, 1))
    preact = jnp.sum(parts.astype(F32), axis=0) * (mine.astype(F32) * (1.0 / WIRE_GAIN))
    active = jax.nn.silu(preact).astype(BF16)
    active = jnp.broadcast_to(active[None], (shares, share_slots, hidden))
    active = lax.all_to_all(active, "pipe", 0, 0, tiled=True).reshape(slots, hidden)
    pieces = pl.pallas_call(
        down_kernel,
        grid=(4,),
        out_shape=jax.ShapeDtypeStruct((slots, width), BF16),
        in_specs=[
            pl.BlockSpec((slots // 4, hidden), lambda i: (i, 0)),
            pl.BlockSpec((width, hidden), lambda i: (0, 0)),
        ],
        out_specs=pl.BlockSpec((slots // 4, width), lambda i: (i, 0)),
        compiler_params=params,
        name="down",
    )(active, down_weight[0].T)
    back = lax.all_to_all(
        pieces.reshape(experts, capacity, width), "expert", 0, 0, tiled=True
    ).reshape(slots, width)
    combined_t = pl.pallas_call(
        combine_kernel,
        out_shape=jax.ShapeDtypeStruct((width, tokens), F32),
        in_specs=[vmem_spec()] * 2,
        out_specs=vmem_spec(),
        compiler_params=params,
        name="combine",
    )(back, gate_slots)
    return combined_t.T


def solution(mesh):
    return jax.shard_map(
        on_device,
        mesh=mesh,
        in_specs=(
            P("expert", "pipe"),
            P("expert"),
            P("expert", None),
            P("expert", None),
            P("expert", "pipe", None),
            P("expert", None, "pipe"),
        ),
        out_specs=P("expert", "pipe"),
        check_vma=False,
    )
```

time: 270 us -> 173 us (0.64)
  the two profiles are of different devices: /device:TPU:6 before, /device:TPU:1 now
where the time goes in v1:
time: 173 us; the launch traced here: 172 us
  blocking collectives  80.6 us (47%)
  waiting for transfers between devices  64.5 us (37%)
  starting transfers between devices  14.2 us (8%)
  Pallas kernels  5.29 us (3%)
  local copies, waits for them, and re-layouts  2.69 us (2%)
  matrix products  2.56 us (1%)
  other arithmetic  2.34 us (1%)
    all_to_all x1, blocking collectives, on_device(): lax.all_to_all(send.reshape(experts, capacity, padded), 'expert', 0, 0, t...  50.1 us
    all_to_all x1, waiting for transfers between devices, on_device(): lax.all_to_all(pieces.reshape(experts, capacity, width), 'expert', 0, 0,...  33.2 us
    all_to_all x1, waiting for transfers between devices, on_device(): lax.all_to_all(terms.reshape(shares, share_slots, hidden), 'pipe', 0, 0,...  31.3 us
    all_to_all x1, blocking collectives, on_device(): lax.all_to_all(active, 'pipe', 0, 0, tiled=True).reshape(slots, hidden)  30.6 us
    all_to_all x1, starting transfers between devices, on_device(): lax.all_to_all(pieces.reshape(experts, capacity, width), 'expert', 0, 0,...  7.39 us
    all_to_all x1, starting transfers between devices, on_device(): lax.all_to_all(terms.reshape(shares, share_slots, hidden), 'pipe', 0, 0,...  6.8 us
  transfers between devices with their start and end apart: 2, of which 2 were waited for; matrix products, arithmetic and copies ran while one was open for 0% of the time, Pallas kernels for 0%

profile of v1, /device:TPU:1, one launch (start us, length us, event | category | flops | bytes accessed | tf_op | source)
XLA Modules:
  0.0 172.2 jit_solution(13292695141237510691)
XLA Ops:
  0.0 0.0 copy-start
  0.0 0.8 reshape.43.scale_ref
  0.8 0.0 copy-start.2
  0.8 0.9 copy-done.2
  1.7 0.0 copy-start.3
  1.7 0.7 copy-done.3
  2.4 0.5 pick.1
  2.9 50.1 %all_to_all.20 = bf16[32,16,512]{2,1,0:T(8,128)(2,1)S(1)} all-to-all(bf16[32,16,512]{2,1,0:T(8,128)(2,1)S(1)} %bitcast.18), channel_id=1, replica_groups=mesh['pipe'=16,'expert'=32] {'expert'}, dimensions={0} | all-to-all | bytes 1048576 | tf_op jit(solution)/shard_map/all_to_all | solution.py:111
  53.0 0.0 copy-done
  53.0 2.6 %multiply_convert_fusion = f16[512,2048]{1,0:T(8,128)(2,1)} fusion(bf16[1,448,2048]{2,1,0:T(8,128)(2,1)S(1)} %copy-done, bf16[512,512]{1,0:T(8,128)(2,1)S(1)} %bitcast.25), kind=kOutput, calls=%fused_computation.1 | convolution fusion | flops 941621248 | bytes 4456448 | tf_op jit(solution)/shard_map/dot_general | solution.py:123
  55.5 6.8 %all-to-all-start.1 = ((f16[16,32,2048]{2,1,0:T(8,128)(2,1)}), f16[16,32,2048]{2,1,0:T(8,128)(2,1)}, u32[]{:S(2)}, u32[]{:S(2)}) async-start(f16[16,32,2048]{2,1,0:T(8,128)(2,1)} %bitcast.24), calls=%async_computation.1 | async-start | bytes 4194304 | tf_op jit(solution)/shard_map/all_to_all | solution.py:125
  62.4 0.2 multiply_reduce_fusion
  62.5 31.3 %all-to-all-done.1 = f16[16,32,2048]{2,1,0:T(8,128)(2,1)} async-done(((f16[16,32,2048]{2,1,0:T(8,128)(2,1)}), f16[16,32,2048]{2,1,0:T(8,128)(2,1)}, u32[]{:S(2)}, u32[]{:S(2)}) %all-to-all-start.1) | async-done | bytes 2097184 | tf_op jit(solution)/shard_map/all_to_all | solution.py:125
  93.8 2.0 %convert_reduce_fusion = f32[32,2048]{1,0:T(8,128)S(1)} fusion(f16[16,32,2048]{2,1,0:T(8,128)(2,1)} %all-to-all-done.1), kind=kLoop, calls=%fused_computation | loop fusion | flops 2031616 | bytes 2359296 | tf_op jit(solution)/shard_map/reduce_sum | solution.py:130
  95.8 0.1 multiply_convert_fusion.1
  96.0 0.2 broadcast_in_dim.2
  96.2 0.0 copy-start.1
  96.2 30.6 %all_to_all.21 = bf16[16,32,2048]{2,1,0:T(8,128)(2,1)S(1)} all-to-all(bf16[16,32,2048]{2,1,0:T(8,128)(2,1)S(1)} %broadcast_in_dim.2), channel_id=1, replica_groups=mesh['pipe'=16,'expert'=32] {'pipe'}, dimensions={0} | all-to-all | bytes 4194304 | tf_op jit(solution)/shard_map/all_to_all | solution.py:133
  126.8 0.0 copy-done.1
  126.8 0.0 copy-start.4
  126.8 0.0 copy-start.5
  126.8 3.4 %down.1 = bf16[512,448]{1,0:T(8,128)(2,1)} custom-call(bf16[512,2048]{1,0:T(8,128)(2,1)S(1)} %bitcast.16, bf16[448,2048]{1,0:T(8,128)(2,1)S(1)} %bitcast.19), custom_call_target="tpu_custom_call" | custom-call | tf_op jit(solution)/shard_map/down/pallas_call | solution.py:134
  130.2 7.4 %all-to-all-start.3 = ((bf16[32,16,448]{2,1,0:T(8,128)(2,1)}), bf16[32,16,448]{2,1,0:T(8,128)(2,1)S(1)}, u32[]{:S(2)}, u32[]{:S(2)}) async-start(bf16[32,16,448]{2,1,0:T(8,128)(2,1)} %bitcast.9), calls=%async_computation.3 | async-start | bytes 1048576 | tf_op jit(solution)/shard_map/all_to_all | solution.py:146
  137.6 0.0 copy-done.4
  137.6 0.0 copy-done.5
  137.7 0.3 gates.1.gate_ref
  138.0 33.2 %all-to-all-done.3 = bf16[32,16,448]{2,1,0:T(8,128)(2,1)S(1)} async-done(((bf16[32,16,448]{2,1,0:T(8,128)(2,1)}), bf16[32,16,448]{2,1,0:T(8,128)(2,1)S(1)}, u32[]{:S(2)}, u32[]{:S(2)}) %all-to-all-start.3) | async-done | bytes 458784 | tf_op jit(solution)/shard_map/all_to_all | solution.py:146
  171.1 1.1 combine.1
Async XLA Ops:
  0.0 53.0 %copy-start = (bf16[1,448,2048]{2,1,0:T(8,128)(2,1)S(1)}, bf16[1,448,2048]{2,1,0:T(8,128)(2,1)}, u32[]{:S(2)}) copy-start(bf16[1,448,2048]{2,1,0:T(8,128)(2,1)} %param.10) | copy-start | bytes 5505028
  0.8 0.9 copy-start.2
  1.7 0.7 copy-start.3
  55.5 38.3 %all-to-all-start.1 = ((f16[16,32,2048]{2,1,0:T(8,128)(2,1)}), f16[16,32,2048]{2,1,0:T(8,128)(2,1)}, u32[]{:S(2)}, u32[]{:S(2)}) async-start(f16[16,32,2048]{2,1,0:T(8,128)(2,1)} %bitcast.24), calls=%async_computation.1 | async-start | bytes 4194304 | tf_op jit(solution)/shard_map/all_to_all | solution.py:125
  96.2 30.6 %copy-start.1 = (bf16[1,2048,448]{1,2,0:T(8,128)(2,1)S(1)}, bf16[1,2048,448]{1,2,0:T(8,128)(2,1)}, u32[]{:S(2)}) copy-start(bf16[1,2048,448]{1,2,0:T(8,128)(2,1)} %param.11) | copy-start | bytes 5505028
  126.8 10.8 %copy-start.4 = (s32[256,8]{0,1:T(8,128)S(1)}, s32[256,8]{0,1:T(8,128)}, u32[]{:S(2)}) copy-start(s32[256,8]{0,1:T(8,128)} %param.8) | copy-start | bytes 24580
  126.8 10.8 %copy-start.5 = (bf16[256,8]{0,1:T(8,128)(2,1)S(1)}, bf16[256,8]{0,1:T(8,128)(2,1)}, u32[]{:S(2)}) copy-start(bf16[256,8]{0,1:T(8,128)(2,1)} %param.9) | copy-start | bytes 12292
  130.2 40.9 %all-to-all-start.3 = ((bf16[32,16,448]{2,1,0:T(8,128)(2,1)}), bf16[32,16,448]{2,1,0:T(8,128)(2,1)S(1)}, u32[]{:S(2)}, u32[]{:S(2)}) async-start(bf16[32,16,448]{2,1,0:T(8,128)(2,1)} %bitcast.9), calls=%async_computation.3 | async-start | bytes 1048576 | tf_op jit(solution)/shard_map/all_to_all | solution.py:146

commit v2 on v1

v2 whole, which is shorter than its diff:
```python
import functools
import math

import jax
import jax.numpy as jnp
from jax import lax
from jax.experimental import pallas as pl
from jax.experimental.pallas import tpu as pltpu
from jax.sharding import PartitionSpec as P

F32 = jnp.float32
BF16 = jnp.bfloat16
WIRE = jnp.float16
WIRE_GAIN = 16.0
ACTIVE_GAIN = 4.0
NT = (((1,), (1,)), ((), ()))
NN = (((1,), (0,)), ((), ()))
TN = (((0,), (0,)), ((), ()))
VMEM_LIMIT = 16 * 1024 * 1024


def vmem_spec():
    return pl.BlockSpec(memory_space=pltpu.VMEM)


def slot_hits(routes_t, experts, capacity):
    tokens = routes_t.shape[1]
    slots = experts * capacity
    expert_id = lax.broadcasted_iota(jnp.int32, (experts, tokens), 0)
    hot = jnp.zeros((experts, tokens), jnp.bool_)
    for k in range(routes_t.shape[0]):
        hot = hot | (routes_t[k : k + 1, :] == expert_id)
    hot_f = jnp.where(hot, 1.0, 0.0)
    before = lax.broadcasted_iota(jnp.int32, (tokens, tokens), 0) < lax.broadcasted_iota(
        jnp.int32, (tokens, tokens), 1
    )
    rank = lax.dot_general(
        hot_f.astype(BF16),
        jnp.where(before, 1.0, 0.0).astype(BF16),
        NN,
        preferred_element_type=F32,
    )
    rank = jnp.where(hot, rank, -1.0)
    rank_slots = jnp.broadcast_to(rank[:, None, :], (experts, capacity, tokens)).reshape(
        slots, tokens
    )
    place = (lax.broadcasted_iota(jnp.int32, (slots, tokens), 0) % capacity).astype(F32)
    return rank_slots == place


def pick_kernel(
    experts, capacity, rows_hbm, scale_hbm, routes_hbm, out_ref, rows_ref, scale_ref, routes_ref, sems
):
    copies = [
        pltpu.make_async_copy(src, dst, sems.at[i])
        for i, (src, dst) in enumerate(
            ((routes_hbm, routes_ref), (scale_hbm, scale_ref), (rows_hbm, rows_ref))
        )
    ]
    for copy in copies:
        copy.start()
    width = rows_ref.shape[0]
    copies[0].wait()
    hits = jnp.where(slot_hits(routes_ref[...], experts, capacity), 1.0, 0.0)
    copies[1].wait()
    scale = scale_ref[...].astype(F32).reshape(1, -1)
    scale = jnp.sum(hits * scale, axis=1, keepdims=True)
    copies[2].wait()
    picked = lax.dot_general(hits.astype(BF16), rows_ref[...], NT, preferred_element_type=F32)
    out_ref[:, :width] = picked.astype(BF16)
    out_ref[:, width:] = jnp.broadcast_to(
        scale.astype(BF16), (out_ref.shape[0], out_ref.shape[1] - width)
    )


def slot_gates(routes_t, gate_t, experts, capacity):
    tokens = routes_t.shape[1]
    expert_id = lax.broadcasted_iota(jnp.int32, (experts, tokens), 0)
    gate = jnp.zeros((experts, tokens), F32)
    for k in range(routes_t.shape[0]):
        gate = jnp.where(
            routes_t[k : k + 1, :] == expert_id, gate_t[k : k + 1, :].astype(F32), gate
        )
    gate_slots = jnp.broadcast_to(gate[:, None, :], (experts, capacity, tokens)).reshape(
        experts * capacity, tokens
    )
    hits = slot_hits(routes_t, experts, capacity)
    return jnp.where(hits, gate_slots, 0.0).astype(BF16)


def pack_kernel(capacity, rows_ref, out_ref):
    width = rows_ref.shape[1]
    whole = width // 128
    half = capacity // 2
    rest = width - whole * 128
    chunks = out_ref.shape[0]
    for j in range(whole):
        out_ref[:, j * capacity : (j + 1) * capacity, :] = rows_ref[
            :, j * 128 : (j + 1) * 128
        ].reshape(chunks, capacity, 128)
    tail = rows_ref[:, whole * 128 :].astype(F32).reshape(chunks, 2, half, rest)
    out_ref[:, whole * capacity :, :] = jnp.concatenate(
        [tail[:, 0], tail[:, 1]], axis=-1
    ).astype(BF16)


def combine_kernel(capacity, width, back_ref, routes_ref, gate_ref, out_ref):
    chunks = back_ref.shape[0]
    whole = width // 128
    half = capacity // 2
    rest = width - whole * 128
    gate = slot_gates(routes_ref[...], gate_ref[...], chunks, capacity)
    for j in range(whole):
        column = back_ref[:, j * capacity : (j + 1) * capacity, :].reshape(chunks * capacity, 128)
        out_ref[j * 128 : (j + 1) * 128, :] = lax.dot_general(
            column, gate, TN, preferred_element_type=F32
        )
    tail = back_ref[:, whole * capacity :, :].astype(F32)
    tail = jnp.stack([tail[:, :, :rest], tail[:, :, rest:]], axis=1)
    tail = tail.reshape(chunks * capacity, rest).astype(BF16)
    out_ref[whole * 128 :, :] = lax.dot_general(tail, gate, TN, preferred_element_type=F32)


def plane_groups(shares, experts, even_along_x):
    side = math.isqrt(shares)
    groups = []
    for expert in range(experts):
        along_x = (expert % 2 == 0) == even_along_x
        for line in range(side):
            shares_here = [line * side + i if along_x else i * side + line for i in range(side)]
            groups.append([share * experts + expert for share in shares_here])
    return groups


def on_device(token_rows, row_scale, routes, gate_weights, up_weight, down_weight):
    experts = lax.axis_size("expert")
    shares = lax.axis_size("pipe")
    tokens, width = token_rows.shape
    hidden = up_weight.shape[2]
    capacity = tokens // 16
    slots = experts * capacity
    padded = -(-(width + 1) // 128) * 128
    params = pltpu.CompilerParams(vmem_limit_bytes=VMEM_LIMIT)
    rows_t = token_rows.T
    routes_t = routes.T
    gate_t = gate_weights.T

    send = pl.pallas_call(
        functools.partial(pick_kernel, experts, capacity),
        out_shape=jax.ShapeDtypeStruct((slots, padded), BF16),
        in_specs=[pl.BlockSpec(memory_space=pltpu.HBM)] * 3,
        out_specs=vmem_spec(),
        scratch_shapes=[
            pltpu.VMEM((width, tokens), BF16),
            pltpu.VMEM((tokens,), BF16),
            pltpu.VMEM(routes_t.shape, jnp.int32),
            pltpu.SemaphoreType.DMA((3,)),
        ],
        name="pick",
    )(rows_t, row_scale, routes_t)
    got = lax.all_to_all(
        send.reshape(experts, capacity, padded), "expert", 0, 0, tiled=True
    ).reshape(slots, padded)
    scale = got[:, width : width + 1].astype(F32) * WIRE_GAIN
    terms = jnp.dot(got[:, :width], up_weight[0], preferred_element_type=F32)
    terms = (terms * scale).astype(WIRE)
    plane = ("pipe", "expert")
    first, second = plane_groups(shares, experts, True), plane_groups(shares, experts, False)
    side = len(first[0])
    side_slots = slots // side
    parts = lax.all_to_all(
        terms.reshape(side, side_slots, hidden), plane, 0, 0, tiled=True, axis_index_groups=first
    )
    partial = jnp.sum(parts.astype(F32), axis=0).astype(WIRE)
    partial = lax.all_gather(partial, plane, axis=0, axis_index_groups=second)
    preact = jnp.sum(partial.astype(F32), axis=0) * (1.0 / WIRE_GAIN)
    active = jax.nn.silu(preact).astype(BF16)
    active = (active.astype(F32) * ACTIVE_GAIN).astype(WIRE)
    active = lax.all_gather(active, plane, axis=0, tiled=True, axis_index_groups=first)
    active = (active.astype(F32) * (1.0 / ACTIVE_GAIN)).astype(BF16)
    pieces = jnp.dot(active, down_weight[0], preferred_element_type=F32).astype(BF16)
    pieces = pl.pallas_call(
        functools.partial(pack_kernel, capacity),
        out_shape=jax.ShapeDtypeStruct((experts, capacity * width // 128, 128), BF16),
        in_specs=[vmem_spec()],
        out_specs=vmem_spec(),
        compiler_params=params,
        name="pack",
    )(pieces)
    back = lax.all_to_all(pieces, "expert", 0, 0, tiled=True)
    combined_t = pl.pallas_call(
        functools.partial(combine_kernel, capacity, width),
        out_shape=jax.ShapeDtypeStruct((width, tokens), F32),
        in_specs=[vmem_spec()] * 3,
        out_specs=vmem_spec(),
        compiler_params=params,
        name="combine",
    )(back, routes_t, gate_t)
    return combined_t.T


def solution(mesh):
    return jax.shard_map(
        on_device,
        mesh=mesh,
        in_specs=(
            P("expert", "pipe"),
            P("expert"),
            P("expert", None),
            P("expert", None),
            P("expert", "pipe", None),
            P("expert", None, "pipe"),
        ),
        out_specs=P("expert", "pipe"),
        check_vma=False,
    )
```

time: 173 us -> 146 us (0.84)
  the two profiles are of different devices: /device:TPU:1 before, /device:TPU:6 now
where the time goes in v2:
time: 146 us; the launch traced here: 143 us
  blocking collectives  135 us (92%)
  Pallas kernels  3.77 us (3%)
  matrix products  2.41 us (2%)
  other arithmetic  1.63 us (1%)
    all_to_all x1, blocking collectives, on_device(): lax.all_to_all(send.reshape(experts, capacity, padded), 'expert', 0, 0, t...  49.3 us
    all_to_all x1, blocking collectives, on_device(): back = lax.all_to_all(pieces, 'expert', 0, 0, tiled=True)  34.2 us
    all_to_all x1, blocking collectives, on_device(): lax.all_to_all(terms.reshape(side, side_slots, hidden), plane, 0, 0, tile...  19 us
    all_gather x1, blocking collectives, on_device(): partial = lax.all_gather(partial, plane, axis=0, axis_index_groups=second)  16.5 us
    all_gather x1, blocking collectives, on_device(): lax.all_gather(active, plane, axis=0, tiled=True, axis_index_groups=first)  16.1 us

profile of v2, /device:TPU:6, one launch (start us, length us, event | category | flops | bytes accessed | tf_op | source)
XLA Modules:
  0.0 143.1 jit_solution(2996041785984300114)
XLA Ops:
  0.0 0.0 copy-start
  0.0 2.4 %pick.1 = bf16[512,512]{1,0:T(8,128)(2,1)} custom-call(bf16[448,256]{1,0:T(8,128)(2,1)} %bitcast.25, bf16[256]{0:T(256)(128)(2,1)} %scale_hbm.1, s32[8,256]{1,0:T(8,128)} %bitcast.17), custom_call_target="tpu_custom_call" | custom-call | tf_op jit(solution)/shard_map/pick/pallas_call | solution.py:148
  2.4 49.3 %all_to_all.15 = bf16[32,16,512]{2,1,0:T(8,128)(2,1)S(1)} all-to-all(bf16[32,16,512]{2,1,0:T(8,128)(2,1)} %bitcast.22), channel_id=1, replica_groups=mesh['pipe'=16,'expert'=32] {'expert'}, dimensions={0} | all-to-all | bytes 1048576 | tf_op jit(solution)/shard_map/all_to_all | solution.py:161
  51.7 0.2 multiply_reduce_fusion
  51.9 0.0 copy-done
  51.9 1.3 multiply_convert_fusion.1
  53.2 19.0 %all_to_all.16 = f16[4,128,2048]{2,1,0:T(8,128)(2,1)S(1)} all-to-all(f16[4,128,2048]{2,1,0:T(8,128)(2,1)S(1)} %bitcast.21), channel_id=1, replica_groups={{0,32,64,96},{128,160,192,224},{256,288,320,352},{384,416,448,480},{1,1..., dimensions={0} | all-to-all | bytes 4194304 | tf_op jit(solution)/shard_map/all_to_all | solution.py:171
  72.2 0.5 convert_reduce_fusion.1
  72.7 0.1 convert_element_type.46
  72.8 16.5 %all-gather.3 = f16[512,2048]{1,0:T(8,128)(2,1)S(1)} all-gather(f16[128,2048]{1,0:T(8,128)(2,1)S(1)} %convert_element_type.46), channel_id=2, replica_groups={{0,128,256,384},{32,160,288,416},{64,192,320,448},{96,224,352,480},{1,3..., dimensions={0}, use_global_device_ids=true | all-gather | bytes 2621440 | tf_op jit(solution)/shard_map/all_gather | solution.py:175
  89.2 0.5 convert_reduce_fusion
  89.7 0.0 copy-start.3
  89.8 0.3 multiply_convert_fusion.5
  90.1 16.1 %all-gather.4 = f16[512,2048]{1,0:T(8,128)(2,1)S(1)} all-gather(f16[128,2048]{1,0:T(8,128)(2,1)S(1)} %multiply_convert_fusion.5), channel_id=1, replica_groups={{0,32,64,96},{128,160,192,224},{256,288,320,352},{384,416,448,480},{1,1..., dimensions={0}, use_global_device_ids=true | all-gather | bytes 2621440 | tf_op jit(solution)/shard_map/all_gather | solution.py:179
  106.2 0.0 copy-done.3
  106.2 1.2 fusion.4
  107.3 0.0 copy-start.1
  107.3 0.0 copy-start.2
  107.3 0.2 copy.12.rows_ref
  107.6 0.1 pack.1
  107.7 34.2 %all_to_all.17.back_ref = bf16[32,56,128]{2,1,0:T(8,128)(2,1)S(1)} all-to-all(bf16[32,56,128]{2,1,0:T(8,128)(2,1)S(1)} %pack.1), channel_id=1, replica_groups=mesh['pipe'=16,'expert'=32] {'expert'}, dimensions={0} | all-to-all | bytes 917504 | tf_op jit(solution)/shard_map/all_to_all | solution.py:190
  141.8 0.0 copy-done.1
  141.8 0.0 copy-done.2
  141.8 1.3 combine.1
Async XLA Ops:
  0.0 51.9 %copy-start = (bf16[1,448,2048]{2,1,0:T(8,128)(2,1)S(1)}, bf16[1,448,2048]{2,1,0:T(8,128)(2,1)}, u32[]{:S(2)}) copy-start(bf16[1,448,2048]{2,1,0:T(8,128)(2,1)} %param.10) | copy-start | bytes 5505028
  89.7 16.4 %copy-start.3 = (bf16[1,2048,448]{1,2,0:T(8,128)(2,1)S(1)}, bf16[1,2048,448]{1,2,0:T(8,128)(2,1)}, u32[]{:S(2)}) copy-start(bf16[1,2048,448]{1,2,0:T(8,128)(2,1)} %param.11) | copy-start | bytes 5505028
  107.3 34.5 %copy-start.1 = (s32[256,8]{0,1:T(8,128)S(1)}, s32[256,8]{0,1:T(8,128)}, u32[]{:S(2)}) copy-start(s32[256,8]{0,1:T(8,128)} %param.8) | copy-start | bytes 24580
  107.3 34.5 %copy-start.2 = (bf16[256,8]{0,1:T(8,128)(2,1)S(1)}, bf16[256,8]{0,1:T(8,128)(2,1)}, u32[]{:S(2)}) copy-start(bf16[256,8]{0,1:T(8,128)(2,1)} %param.9) | copy-start | bytes 12292

commit v3 on v2

--- a/solution.py
+++ b/solution.py
@@ -16,7 +16,12 @@
 NT = (((1,), (1,)), ((), ()))
 NN = (((1,), (0,)), ((), ()))
 TN = (((0,), (0,)), ((), ()))
-VMEM_LIMIT = 16 * 1024 * 1024
+TILE = 512
+VMEM_LIMIT = 24 * 1024 * 1024
+
+
+def relabel(routes):
+    return routes ^ (lax.axis_index("expert") % 2)
 
 
 def vmem_spec():
@@ -61,7 +66,7 @@
         copy.start()
     width = rows_ref.shape[0]
     copies[0].wait()
-    hits = jnp.where(slot_hits(routes_ref[...], experts, capacity), 1.0, 0.0)
+    hits = jnp.where(slot_hits(relabel(routes_ref[...]), experts, capacity), 1.0, 0.0)
     copies[1].wait()
     scale = scale_ref[...].astype(F32).reshape(1, -1)
     scale = jnp.sum(hits * scale, axis=1, keepdims=True)
@@ -88,20 +93,44 @@
     return jnp.where(hits, gate_slots, 0.0).astype(BF16)
 
 
-def pack_kernel(capacity, rows_ref, out_ref):
-    width = rows_ref.shape[1]
+def pair_kernel(own_ref, other_ref, later_ref, out_ref, mark_ref):
+    out_ref[0] = own_ref[...]
+    out_ref[1] = other_ref[...]
+    mark_ref[...] = jnp.zeros(mark_ref.shape, F32)
+
+
+def join_kernel(got_ref, mark_ref, out_ref):
+    out_ref[...] = mark_ref[...]
+
+
+def up_kernel(capacity, got_ref, weight_ref, out_ref):
+    width, hidden = weight_ref.shape[1:]
+    slots = got_ref.shape[0] * capacity
+    for i in range(2):
+        rows = got_ref[:, i * capacity : (i + 1) * capacity, :].reshape(slots, got_ref.shape[2])
+        scale = rows[:, width : width + 1].astype(F32) * WIRE_GAIN
+        rows = rows[:, :width]
+        for j in range(0, hidden, TILE):
+            term = jnp.dot(rows, weight_ref[i, :, j : j + TILE], preferred_element_type=F32)
+            out_ref[i * slots : (i + 1) * slots, j : j + TILE] = term * scale
+
+
+def down_kernel(capacity, own_ref, active_ref, weight_ref, out_ref):
+    width = weight_ref.shape[0]
     whole = width // 128
     half = capacity // 2
     rest = width - whole * 128
     chunks = out_ref.shape[0]
-    for j in range(whole):
-        out_ref[:, j * capacity : (j + 1) * capacity, :] = rows_ref[
-            :, j * 128 : (j + 1) * 128
-        ].reshape(chunks, capacity, 128)
-    tail = rows_ref[:, whole * 128 :].astype(F32).reshape(chunks, 2, half, rest)
-    out_ref[:, whole * capacity :, :] = jnp.concatenate(
-        [tail[:, 0], tail[:, 1]], axis=-1
-    ).astype(BF16)
+    other = lax.dot_general(active_ref[...], weight_ref[...], NT, preferred_element_type=F32)
+    for i, piece in enumerate((own_ref[...].astype(F32), other)):
+        for j in range(whole):
+            out_ref[:, i, j * capacity : (j + 1) * capacity, :] = (
+                piece[:, j * 128 : (j + 1) * 128].astype(BF16).reshape(chunks, capacity, 128)
+            )
+        tail = piece[:, whole * 128 :].reshape(chunks, 2, half, rest)
+        out_ref[:, i, whole * capacity :, :] = jnp.concatenate(
+            [tail[:, 0], tail[:, 1]], axis=-1
+        ).astype(BF16)
 
 
 def combine_kernel(capacity, width, back_ref, routes_ref, gate_ref, out_ref):
@@ -109,7 +138,7 @@
     whole = width // 128
     half = capacity // 2
     rest = width - whole * 128
-    gate = slot_gates(routes_ref[...], gate_ref[...], chunks, capacity)
+    gate = slot_gates(relabel(routes_ref[...]), gate_ref[...], chunks, capacity)
     for j in range(whole):
         column = back_ref[:, j * capacity : (j + 1) * capacity, :].reshape(chunks * capacity, 128)
         out_ref[j * 128 : (j + 1) * 128, :] = lax.dot_general(
@@ -158,12 +187,47 @@
         ],
         name="pick",
     )(rows_t, row_scale, routes_t)
+    chips = experts // 2
+    rings = [[2 * chip + core for chip in range(chips)] for core in range(2)]
+    swap = [(i, i ^ 1) for i in range(experts)]
+    up_own, down_own = up_weight[0], down_weight[0].T
+    up_other = lax.ppermute(up_own, "expert", swap)
+    down_other = lax.ppermute(down_own, "expert", swap)
     got = lax.all_to_all(
-        send.reshape(experts, capacity, padded), "expert", 0, 0, tiled=True
-    ).reshape(slots, padded)
-    scale = got[:, width : width + 1].astype(F32) * WIRE_GAIN
-    terms = jnp.dot(got[:, :width], up_weight[0], preferred_element_type=F32)
-    terms = (terms * scale).astype(WIRE)
+        send.reshape(chips, 2 * capacity, padded), "expert", 0, 0, tiled=True,
+        axis_index_groups=rings,
+    )
+    anywhere = pl.BlockSpec(memory_space=pl.ANY)
+    up_both, mark = pl.pallas_call(
+        pair_kernel,
+        out_shape=[
+            jax.ShapeDtypeStruct((2, width, hidden), BF16),
+            jax.ShapeDtypeStruct((8, hidden), F32),
+        ],
+        in_specs=[vmem_spec(), vmem_spec(), anywhere],
+        out_specs=[vmem_spec()] * 2,
+        compiler_params=params,
+        cost_estimate=pl.CostEstimate(flops=0, bytes_accessed=100000, transcendentals=0),
+        name="pair",
+    )(up_own, up_other, down_other)
+    after = pl.pallas_call(
+        join_kernel,
+        out_shape=jax.ShapeDtypeStruct((8, hidden), F32),
+        in_specs=[anywhere, vmem_spec()],
+        out_specs=vmem_spec(),
+        compiler_params=params,
+        name="join",
+    )(got, mark)
+    after = lax.ppermute(after, "expert", swap)
+    terms = pl.pallas_call(
+        functools.partial(up_kernel, capacity),
+        out_shape=jax.ShapeDtypeStruct((slots, hidden), F32),
+        in_specs=[vmem_spec()] * 2,
+        out_specs=vmem_spec(),
+        compiler_params=params,
+        name="up",
+    )(got, up_both)
+    terms = (terms + after[:1]).astype(WIRE)
     plane = ("pipe", "expert")
     first, second = plane_groups(shares, experts, True), plane_groups(shares, experts, False)
     side = len(first[0])
@@ -177,17 +241,22 @@
     active = jax.nn.silu(preact).astype(BF16)
     active = (active.astype(F32) * ACTIVE_GAIN).astype(WIRE)
     active = lax.all_gather(active, plane, axis=0, tiled=True, axis_index_groups=first)
-    active = (active.astype(F32) * (1.0 / ACTIVE_GAIN)).astype(BF16)
-    pieces = jnp.dot(active, down_weight[0], preferred_element_type=F32).astype(BF16)
+    own, other = (
+        (rows.astype(F32) * (1.0 / ACTIVE_GAIN)).astype(BF16) for rows in jnp.split(active, 2)
+    )
+    own = lax.dot_general(own, down_own, NT, preferred_element_type=F32).astype(BF16)
+    packed = capacity * width // 128
     pieces = pl.pallas_call(
-        functools.partial(pack_kernel, capacity),
-        out_shape=jax.ShapeDtypeStruct((experts, capacity * width // 128, 128), BF16),
-        in_specs=[vmem_spec()],
-        out_specs=vmem_spec(),
-        compiler_params=params,
-        name="pack",
-    )(pieces)
-    back = lax.all_to_all(pieces, "expert", 0, 0, tiled=True)
+        functools.partial(down_kernel, capacity),
+        out_shape=jax.ShapeDtypeStruct((chips, 2, packed, 128), BF16),
+        in_specs=[vmem_spec()] * 3,
+        out_specs=vmem_spec(),
+        compiler_params=params,
+        name="down",
+    )(own, other, down_other)
+    back = lax.all_to_all(
+        pieces.reshape(chips, 2 * packed, 128), "expert", 0, 0, tiled=True, axis_index_groups=rings
+    ).reshape(experts, packed, 128)
     combined_t = pl.pallas_call(
         functools.partial(combine_kernel, capacity, width),
         out_shape=jax.ShapeDtypeStruct((width, tokens), F32),

time: 146 us -> 138 us (0.945); the launches traced: 143 us -> 137 us
  blocking collectives: 135 us -> 80.4 us
  starting transfers between devices: 0 us -> 21.4 us
  waiting for transfers between devices: 0 us -> 21.2 us
  local copies, waits for them, and re-layouts: 0.23 us -> 5.48 us
  Pallas kernels: 3.77 us -> 5.84 us
  matrix products: 2.41 us -> 0.68 us
    all_to_all x2 -> x1, blocking collectives: 83.4 us -> 28.9 us  [on_device(): lax.all_to_all(pieces.reshape(chips, 2 * packed, 128), 'expert', 0, 0, ti...]
    all_to_all x0 -> x1, waiting for transfers between devices: none -> 17 us  [on_device(): lax.all_to_all(send.reshape(chips, 2 * capacity, padded), 'expert', 0, 0,...]
    all_to_all x0 -> x1, starting transfers between devices: none -> 15.2 us  [on_device(): lax.all_to_all(send.reshape(chips, 2 * capacity, padded), 'expert', 0, 0,...]
    ppermute x0 -> x3, starting transfers between devices: none -> 6.24 us  [the longest x1 2.41 us: on_device(): down_other = lax.ppermute(down_own, 'expert', swap)]
    unnamed x8 -> x12, local copies, waits for them, and re-layouts: 0.02 us -> 5.33 us
    ppermute x0 -> x3, waiting for transfers between devices: none -> 4.17 us  [the longest x1 2.62 us: on_device(): down_other = lax.ppermute(down_own, 'expert', swap)]
    pallas_call x1 -> x4, Pallas kernels: 0.1 us -> 2.29 us  [the longest x1 1.26 us: on_device(): pl.pallas_call(functools.partial(up_kernel, capacity), out_shape=jax.Shap...]
    dot_general x2 -> x1, matrix products: 2.41 us -> 0.68 us  [on_device(): lax.dot_general(own, down_own, NT, preferred_element_type=F32).astype(BF16)]
  transfers between devices with their start and end apart: 0 -> 4, of which waited for: 0 -> 3; matrix products, arithmetic and copies ran while one was open for 0% -> 0% of each run, Pallas kernels for 0% -> 1%
where the time goes in v3:
time: 138 us; the launch traced here: 137 us
  blocking collectives  80.4 us (58%)
  starting transfers between devices  21.4 us (16%)
  waiting for transfers between devices  21.2 us (15%)
  Pallas kernels  5.84 us (4%)
  local copies, waits for them, and re-layouts  5.48 us (4%)
  other arithmetic  2.17 us (2%)
    all_to_all x1, blocking collectives, on_device(): lax.all_to_all(pieces.reshape(chips, 2 * packed, 128), 'expert', 0, 0, ti...  28.9 us
    all_to_all x1, blocking collectives, on_device(): lax.all_to_all(terms.reshape(side, side_slots, hidden), plane, 0, 0, tile...  19 us
    all_to_all x1, waiting for transfers between devices, on_device(): lax.all_to_all(send.reshape(chips, 2 * capacity, padded), 'expert', 0, 0,...  17 us
    all_gather x1, blocking collectives, on_device(): partial = lax.all_gather(partial, plane, axis=0, axis_index_groups=second)  16.5 us
    all_gather x1, blocking collectives, on_device(): lax.all_gather(active, plane, axis=0, tiled=True, axis_index_groups=first)  16.1 us
    all_to_all x1, starting transfers between devices, on_device(): lax.all_to_all(send.reshape(chips, 2 * capacity, padded), 'expert', 0, 0,...  15.2 us
    unnamed x12, local copies, waits for them, and re-layouts  5.33 us
  transfers between devices with their start and end apart: 4, of which 3 were waited for; matrix products, arithmetic and copies ran while one was open for 0% of the time, Pallas kernels for 1%

profile of v3, /device:TPU:6, one launch (start us, length us, event | category | flops | bytes accessed | tf_op | source)
XLA Modules:
  0.0 137.4 jit_solution(16185864375090330473)
XLA Ops:
  0.0 2.3 %pick.1 = bf16[512,512]{1,0:T(8,128)(2,1)} custom-call(bf16[448,256]{1,0:T(8,128)(2,1)} %bitcast.29, bf16[256]{0:T(256)(128)(2,1)} %scale_hbm.1, s32[8,256]{1,0:T(8,128)} %bitcast.23), custom_call_target="tpu_custom_call" | custom-call | tf_op jit(solution)/shard_map/pick/pallas_call | solution.py:177
  2.3 15.2 %all-to-all-start = ((bf16[16,32,512]{2,1,0:T(8,128)(2,1)}), bf16[16,32,512]{2,1,0:T(8,128)(2,1)S(1)}, u32[]{:S(2)}, u32[]{:S(2)}) async-start(bf16[16,32,512]{2,1,0:T(8,128)(2,1)} %bitcast.28), calls=%async_computation | async-start | bytes 1048576 | tf_op jit(solution)/shard_map/all_to_all | solution.py:196
  17.5 1.9 %collective-permute-start = (bf16[448,2048]{1,0:T(8,128)(2,1)}, bf16[448,2048]{1,0:T(8,128)(2,1)S(1)}, u32[]{:S(2)}, u32[]{:S(2)}) collective-permute-start(bf16[448,2048]{1,0:T(8,128)(2,1)} %bitcast.21), channel_id=1, source_target_pairs={{0,1},{1,0},{2,3},{3,2},{4,5},{5,4},{6,7},{7,6},{8,9},{9,8},{10,11... | collective-permute-start | bytes 5505032 | tf_op jit(solution)/shard_map/ppermute | solution.py:194
  19.4 2.4 %collective-permute-start.1 = (bf16[448,2048]{1,0:T(8,128)(2,1)}, bf16[448,2048]{1,0:T(8,128)(2,1)S(1)}, u32[]{:S(2)}, u32[]{:S(2)}) collective-permute-start(bf16[448,2048]{1,0:T(8,128)(2,1)} %bitcast.31), channel_id=1, source_target_pairs={{0,1},{1,0},{2,3},{3,2},{4,5},{5,4},{6,7},{7,6},{8,9},{9,8},{10,11... | collective-permute-start | bytes 5505032 | tf_op jit(solution)/shard_map/ppermute | solution.py:195
  21.8 1.5 %collective-permute-done.other_ref = bf16[448,2048]{1,0:T(8,128)(2,1)S(1)} collective-permute-done((bf16[448,2048]{1,0:T(8,128)(2,1)}, bf16[448,2048]{1,0:T(8,128)(2,1)S(1)}, u32[]{:S(2)}, u32[]{:S(2)}) %collective-permute-start) | collective-permute-done | bytes 1835040 | tf_op jit(solution)/shard_map/ppermute | solution.py:194
  23.4 2.6 %collective-permute-done.1.later_ref.weight_ref = bf16[448,2048]{1,0:T(8,128)(2,1)S(1)} collective-permute-done((bf16[448,2048]{1,0:T(8,128)(2,1)}, bf16[448,2048]{1,0:T(8,128)(2,1)S(1)}, u32[]{:S(2)}, u32[]{:S(2)}) %collective-permute-start.1) | collective-permute-done | bytes 1835040 | tf_op jit(solution)/shard_map/ppermute | solution.py:195
  26.0 0.0 copy-start.2
  26.0 1.5 %copy-done.2 = bf16[1,448,2048]{2,1,0:T(8,128)(2,1)S(1)} copy-done((bf16[1,448,2048]{2,1,0:T(8,128)(2,1)S(1)}, bf16[1,448,2048]{2,1,0:T(8,128)(2,1)}, u32[]{:S(2)}) %copy-start.2) | copy-done | bytes 1835032
  27.5 0.2 pair.1
  27.7 0.0 copy-start
  27.8 1.8 %copy-done = bf16[2,448,2048]{2,1,0:T(8,128)(2,1)} copy-done((bf16[2,448,2048]{2,1,0:T(8,128)(2,1)}, bf16[2,448,2048]{2,1,0:T(8,128)(2,1)S(1)}, u32[]{:S(2)}) %copy-start) | copy-done | bytes 3670040
  29.5 17.0 %all-to-all-done.got_ref = bf16[16,32,512]{2,1,0:T(8,128)(2,1)S(1)} async-done(((bf16[16,32,512]{2,1,0:T(8,128)(2,1)}), bf16[16,32,512]{2,1,0:T(8,128)(2,1)S(1)}, u32[]{:S(2)}, u32[]{:S(2)}) %all-to-all-start) | async-done | bytes 524320 | tf_op jit(solution)/shard_map/all_to_all | solution.py:196
  46.6 1.9 %collective-permute-start.2 = (f32[8,2048]{1,0:T(8,128)S(1)}, f32[8,2048]{1,0:T(8,128)S(1)}, u32[]{:S(2)}, u32[]{:S(2)}) collective-permute-start(f32[8,2048]{1,0:T(8,128)S(1)} %join.1), channel_id=1, source_target_pairs={{0,1},{1,0},{2,3},{3,2},{4,5},{5,4},{6,7},{7,6},{8,9},{9,8},{10,11... | collective-permute-start | bytes 196616 | tf_op jit(solution)/shard_map/ppermute | solution.py:221
  48.5 0.0 copy-start.1
  48.5 2.0 %copy-done.1 = bf16[2,448,2048]{2,1,0:T(8,128)(2,1)S(1)} copy-done((bf16[2,448,2048]{2,1,0:T(8,128)(2,1)S(1)}, bf16[2,448,2048]{2,1,0:T(8,128)(2,1)}, u32[]{:S(2)}) %copy-start.1) | copy-done | bytes 3670040
  50.5 1.3 up.1
  51.8 0.0 collective-permute-done.2
  51.8 0.5 add_convert_fusion
  52.4 19.0 %all_to_all.15 = f16[4,128,2048]{2,1,0:T(8,128)(2,1)S(1)} all-to-all(f16[4,128,2048]{2,1,0:T(8,128)(2,1)S(1)} %bitcast.27), channel_id=1, replica_groups={{0,32,64,96},{128,160,192,224},{256,288,320,352},{384,416,448,480},{1,1..., dimensions={0} | all-to-all | bytes 4194304 | tf_op jit(solution)/shard_map/all_to_all | solution.py:235
  71.4 0.5 convert_reduce_fusion.1
  71.9 0.1 convert_element_type.48
  72.0 16.5 %all-gather.3 = f16[512,2048]{1,0:T(8,128)(2,1)S(1)} all-gather(f16[128,2048]{1,0:T(8,128)(2,1)S(1)} %convert_element_type.48), channel_id=2, replica_groups={{0,128,256,384},{32,160,288,416},{64,192,320,448},{96,224,352,480},{1,3..., dimensions={0}, use_global_device_ids=true | all-gather | bytes 2621440 | tf_op jit(solution)/shard_map/all_gather | solution.py:239
  88.4 0.5 convert_reduce_fusion
  89.0 0.0 copy-start.5
  89.0 0.3 multiply_convert_fusion.3
  89.3 16.1 %all-gather.4 = f16[512,2048]{1,0:T(8,128)(2,1)S(1)} all-gather(f16[128,2048]{1,0:T(8,128)(2,1)S(1)} %multiply_convert_fusion.3), channel_id=1, replica_groups={{0,32,64,96},{128,160,192,224},{256,288,320,352},{384,416,448,480},{1,1..., dimensions={0}, use_global_device_ids=true | all-gather | bytes 2621440 | tf_op jit(solution)/shard_map/all_gather | solution.py:243
  105.4 0.0 copy-done.5
  105.4 0.7 fusion.2
  106.1 0.2 multiply_convert_fusion.active_ref
  106.3 0.1 copy.9.own_ref
  106.5 0.0 copy-start.3
  106.5 0.0 copy-start.4
  106.5 0.8 down.1
  107.3 28.9 %all_to_all.16 = bf16[16,112,128]{2,1,0:T(8,128)(2,1)S(1)} all-to-all(bf16[16,112,128]{2,1,0:T(8,128)(2,1)S(1)} %bitcast.19), channel_id=1, replica_groups={{0,2,4,6,8,10,12,14,16,18,20,22,24,26,28,30},{1,3,5,7,9,11,13,15,17,19,..., dimensions={0} | all-to-all | bytes 917504 | tf_op jit(solution)/shard_map/all_to_all | solution.py:257
  136.1 0.0 copy-done.3
  136.1 0.0 copy-done.4
  136.1 1.3 combine.1
  (2 shorter events, 0.0 us)
Async XLA Ops:
  2.3 44.3 %all-to-all-start = ((bf16[16,32,512]{2,1,0:T(8,128)(2,1)}), bf16[16,32,512]{2,1,0:T(8,128)(2,1)S(1)}, u32[]{:S(2)}, u32[]{:S(2)}) async-start(bf16[16,32,512]{2,1,0:T(8,128)(2,1)} %bitcast.28), calls=%async_computation | async-start | bytes 1048576 | tf_op jit(solution)/shard_map/all_to_all | solution.py:196
  17.5 5.9 %collective-permute-start = (bf16[448,2048]{1,0:T(8,128)(2,1)}, bf16[448,2048]{1,0:T(8,128)(2,1)S(1)}, u32[]{:S(2)}, u32[]{:S(2)}) collective-permute-start(bf16[448,2048]{1,0:T(8,128)(2,1)} %bitcast.21), channel_id=1, source_target_pairs={{0,1},{1,0},{2,3},{3,2},{4,5},{5,4},{6,7},{7,6},{8,9},{9,8},{10,11... | collective-permute-start | bytes 5505032 | tf_op jit(solution)/shard_map/ppermute | solution.py:194
  19.4 6.6 %collective-permute-start.1 = (bf16[448,2048]{1,0:T(8,128)(2,1)}, bf16[448,2048]{1,0:T(8,128)(2,1)S(1)}, u32[]{:S(2)}, u32[]{:S(2)}) collective-permute-start(bf16[448,2048]{1,0:T(8,128)(2,1)} %bitcast.31), channel_id=1, source_target_pairs={{0,1},{1,0},{2,3},{3,2},{4,5},{5,4},{6,7},{7,6},{8,9},{9,8},{10,11... | collective-permute-start | bytes 5505032 | tf_op jit(solution)/shard_map/ppermute | solution.py:195
  26.0 1.5 %copy-start.2 = (bf16[1,448,2048]{2,1,0:T(8,128)(2,1)S(1)}, bf16[1,448,2048]{2,1,0:T(8,128)(2,1)}, u32[]{:S(2)}) copy-start(bf16[1,448,2048]{2,1,0:T(8,128)(2,1)} %param.10) | copy-start | bytes 5505028
  27.7 1.8 %copy-start = (bf16[2,448,2048]{2,1,0:T(8,128)(2,1)}, bf16[2,448,2048]{2,1,0:T(8,128)(2,1)S(1)}, u32[]{:S(2)}) copy-start(bf16[2,448,2048]{2,1,0:T(8,128)(2,1)S(1)} %get-tuple-element.7.weight_ref) | copy-start | bytes 11010052
  46.6 5.2 %collective-permute-start.2 = (f32[8,2048]{1,0:T(8,128)S(1)}, f32[8,2048]{1,0:T(8,128)S(1)}, u32[]{:S(2)}, u32[]{:S(2)}) collective-permute-start(f32[8,2048]{1,0:T(8,128)S(1)} %join.1), channel_id=1, source_target_pairs={{0,1},{1,0},{2,3},{3,2},{4,5},{5,4},{6,7},{7,6},{8,9},{9,8},{10,11... | collective-permute-start | bytes 196616 | tf_op jit(solution)/shard_map/ppermute | solution.py:221
  48.5 2.0 %copy-start.1 = (bf16[2,448,2048]{2,1,0:T(8,128)(2,1)S(1)}, bf16[2,448,2048]{2,1,0:T(8,128)(2,1)}, u32[]{:S(2)}) copy-start(bf16[2,448,2048]{2,1,0:T(8,128)(2,1)} %copy-done) | copy-start | bytes 11010052
  89.0 16.4 %copy-start.5 = (bf16[1,2048,448]{1,2,0:T(8,128)(2,1)S(1)}, bf16[1,2048,448]{1,2,0:T(8,128)(2,1)}, u32[]{:S(2)}) copy-start(bf16[1,2048,448]{1,2,0:T(8,128)(2,1)} %param.11) | copy-start | bytes 5505028
  106.5 29.7 %copy-start.3 = (s32[256,8]{0,1:T(8,128)S(1)}, s32[256,8]{0,1:T(8,128)}, u32[]{:S(2)}) copy-start(s32[256,8]{0,1:T(8,128)} %param.8) | copy-start | bytes 24580
  106.5 29.7 %copy-start.4 = (bf16[256,8]{0,1:T(8,128)(2,1)S(1)}, bf16[256,8]{0,1:T(8,128)(2,1)}, u32[]{:S(2)}) copy-start(bf16[256,8]{0,1:T(8,128)(2,1)} %param.9) | copy-start | bytes 12292

commit v4 on v3

--- a/solution.py
+++ b/solution.py
@@ -93,25 +93,23 @@
     return jnp.where(hits, gate_slots, 0.0).astype(BF16)
 
 
-def pair_kernel(own_ref, other_ref, later_ref, out_ref, mark_ref):
-    out_ref[0] = own_ref[...]
-    out_ref[1] = other_ref[...]
-    mark_ref[...] = jnp.zeros(mark_ref.shape, F32)
-
-
-def join_kernel(got_ref, mark_ref, out_ref):
-    out_ref[...] = mark_ref[...]
-
-
-def up_kernel(capacity, got_ref, weight_ref, out_ref):
-    width, hidden = weight_ref.shape[1:]
+def join_kernel(got_ref, later_ref, out_ref):
+    out_ref[...] = jnp.zeros(out_ref.shape, F32)
+
+
+def up_kernel(capacity, got_ref, own_ref, other_hbm, out_ref, other_ref, sem):
+    copy = pltpu.make_async_copy(other_hbm, other_ref, sem)
+    copy.start()
+    width, hidden = own_ref.shape
     slots = got_ref.shape[0] * capacity
-    for i in range(2):
+    for i, weight_ref in enumerate((own_ref, other_ref)):
+        if i == 1:
+            copy.wait()
         rows = got_ref[:, i * capacity : (i + 1) * capacity, :].reshape(slots, got_ref.shape[2])
         scale = rows[:, width : width + 1].astype(F32) * WIRE_GAIN
         rows = rows[:, :width]
         for j in range(0, hidden, TILE):
-            term = jnp.dot(rows, weight_ref[i, :, j : j + TILE], preferred_element_type=F32)
+            term = jnp.dot(rows, weight_ref[:, j : j + TILE], preferred_element_type=F32)
             out_ref[i * slots : (i + 1) * slots, j : j + TILE] = term * scale
 
 
@@ -198,35 +196,24 @@
         axis_index_groups=rings,
     )
     anywhere = pl.BlockSpec(memory_space=pl.ANY)
-    up_both, mark = pl.pallas_call(
-        pair_kernel,
-        out_shape=[
-            jax.ShapeDtypeStruct((2, width, hidden), BF16),
-            jax.ShapeDtypeStruct((8, hidden), F32),
-        ],
-        in_specs=[vmem_spec(), vmem_spec(), anywhere],
-        out_specs=[vmem_spec()] * 2,
-        compiler_params=params,
-        cost_estimate=pl.CostEstimate(flops=0, bytes_accessed=100000, transcendentals=0),
-        name="pair",
-    )(up_own, up_other, down_other)
     after = pl.pallas_call(
         join_kernel,
         out_shape=jax.ShapeDtypeStruct((8, hidden), F32),
-        in_specs=[anywhere, vmem_spec()],
+        in_specs=[anywhere] * 2,
         out_specs=vmem_spec(),
         compiler_params=params,
         name="join",
-    )(got, mark)
+    )(got, down_other)
     after = lax.ppermute(after, "expert", swap)
     terms = pl.pallas_call(
         functools.partial(up_kernel, capacity),
         out_shape=jax.ShapeDtypeStruct((slots, hidden), F32),
-        in_specs=[vmem_spec()] * 2,
-        out_specs=vmem_spec(),
+        in_specs=[vmem_spec(), vmem_spec(), anywhere],
+        out_specs=vmem_spec(),
+        scratch_shapes=[pltpu.VMEM((width, hidden), BF16), pltpu.SemaphoreType.DMA],
         compiler_params=params,
         name="up",
-    )(got, up_both)
+    )(got, up_own, up_other)
     terms = (terms + after[:1]).astype(WIRE)
     plane = ("pipe", "expert")
     first, second = plane_groups(shares, experts, True), plane_groups(shares, experts, False)
@@ -235,9 +222,9 @@
     parts = lax.all_to_all(
         terms.reshape(side, side_slots, hidden), plane, 0, 0, tiled=True, axis_index_groups=first
     )
-    partial = jnp.sum(parts.astype(F32), axis=0).astype(WIRE)
+    partial = sum(parts[i].astype(F32) for i in range(side)).astype(WIRE)
     partial = lax.all_gather(partial, plane, axis=0, axis_index_groups=second)
-    preact = jnp.sum(partial.astype(F32), axis=0) * (1.0 / WIRE_GAIN)
+    preact = sum(partial[i].astype(F32) for i in range(side)) * (1.0 / WIRE_GAIN)
     active = jax.nn.silu(preact).astype(BF16)
     active = (active.astype(F32) * ACTIVE_GAIN).astype(WIRE)
     active = lax.all_gather(active, plane, axis=0, tiled=True, axis_index_groups=first)

time: 138 us -> 137 us (level)
  local copies, waits for them, and re-layouts: 5.48 us -> 0.17 us
  waiting for transfers between devices: 21.2 us -> 24.7 us
    all_to_all x1, waiting for transfers between devices: 17 us -> 23.2 us  [on_device(): lax.all_to_all(send.reshape(chips, 2 * capacity, padded), 'expert', 0, 0,...]
    unnamed x12 -> x8, local copies, waits for them, and re-layouts: 5.33 us -> 0.02 us
    ppermute x1, waiting for transfers between devices: 1.54 us -> 0.01 us  [on_device(): up_other = lax.ppermute(up_own, 'expert', swap)]
  transfers between devices with their start and end apart: 4 -> 4, of which waited for: 3 -> 2; matrix products, arithmetic and copies ran while one was open for 0% -> 0% of each run, Pallas kernels for 1% -> 2%
where the time goes in v4:
time: 137 us; the launch traced here: 136 us
  blocking collectives  80.4 us (59%)
  waiting for transfers between devices  24.7 us (18%)
  starting transfers between devices  21.6 us (16%)
  Pallas kernels  6.56 us (5%)
  other arithmetic  1.75 us (1%)
    all_to_all x1, blocking collectives, on_device(): lax.all_to_all(pieces.reshape(chips, 2 * packed, 128), 'expert', 0, 0, ti...  28.9 us
    all_to_all x1, waiting for transfers between devices, on_device(): lax.all_to_all(send.reshape(chips, 2 * capacity, padded), 'expert', 0, 0,...  23.2 us
    all_to_all x1, blocking collectives, on_device(): lax.all_to_all(terms.reshape(side, side_slots, hidden), plane, 0, 0, tile...  19 us
    all_gather x1, blocking collectives, on_device(): partial = lax.all_gather(partial, plane, axis=0, axis_index_groups=second)  16.5 us
    all_gather x1, blocking collectives, on_device(): lax.all_gather(active, plane, axis=0, tiled=True, axis_index_groups=first)  16.1 us
    all_to_all x1, starting transfers between devices, on_device(): lax.all_to_all(send.reshape(chips, 2 * capacity, padded), 'expert', 0, 0,...  15.2 us
  transfers between devices with their start and end apart: 4, of which 2 were waited for; matrix products, arithmetic and copies ran while one was open for 0% of the time, Pallas kernels for 2%

profile of v4, /device:TPU:6, one launch (start us, length us, event | category | flops | bytes accessed | tf_op | source)
XLA Modules:
  0.0 136.1 jit_solution(6658213164597306778)
XLA Ops:
  0.0 2.3 %pick.1 = bf16[512,512]{1,0:T(8,128)(2,1)} custom-call(bf16[448,256]{1,0:T(8,128)(2,1)} %bitcast.41, bf16[256]{0:T(256)(128)(2,1)} %scale_hbm.1, s32[8,256]{1,0:T(8,128)} %bitcast.36), custom_call_target="tpu_custom_call" | custom-call | tf_op jit(solution)/shard_map/pick/pallas_call | solution.py:175
  2.3 15.2 %all-to-all-start = ((bf16[16,32,512]{2,1,0:T(8,128)(2,1)}), bf16[16,32,512]{2,1,0:T(8,128)(2,1)S(1)}, u32[]{:S(2)}, u32[]{:S(2)}) async-start(bf16[16,32,512]{2,1,0:T(8,128)(2,1)} %bitcast.40), calls=%async_computation | async-start | bytes 1048576 | tf_op jit(solution)/shard_map/all_to_all | solution.py:194
  17.5 1.9 %collective-permute-start.1 = (bf16[448,2048]{1,0:T(8,128)(2,1)}, bf16[448,2048]{1,0:T(8,128)(2,1)S(1)}, u32[]{:S(2)}, u32[]{:S(2)}) collective-permute-start(bf16[448,2048]{1,0:T(8,128)(2,1)} %bitcast.43), channel_id=1, source_target_pairs={{0,1},{1,0},{2,3},{3,2},{4,5},{5,4},{6,7},{7,6},{8,9},{9,8},{10,11... | collective-permute-start | bytes 5505032 | tf_op jit(solution)/shard_map/ppermute | solution.py:193
  19.4 2.4 %collective-permute-start = (bf16[448,2048]{1,0:T(8,128)(2,1)}, bf16[448,2048]{1,0:T(8,128)(2,1)}, u32[]{:S(2)}, u32[]{:S(2)}) collective-permute-start(bf16[448,2048]{1,0:T(8,128)(2,1)} %bitcast.34), channel_id=1, source_target_pairs={{0,1},{1,0},{2,3},{3,2},{4,5},{5,4},{6,7},{7,6},{8,9},{9,8},{10,11... | collective-permute-start | bytes 5505032 | tf_op jit(solution)/shard_map/ppermute | solution.py:192
  21.8 1.5 %collective-permute-done.1.later_ref.weight_ref = bf16[448,2048]{1,0:T(8,128)(2,1)S(1)} collective-permute-done((bf16[448,2048]{1,0:T(8,128)(2,1)}, bf16[448,2048]{1,0:T(8,128)(2,1)S(1)}, u32[]{:S(2)}, u32[]{:S(2)}) %collective-permute-start.1) | collective-permute-done | bytes 1835040 | tf_op jit(solution)/shard_map/ppermute | solution.py:193
  23.4 23.2 %all-to-all-done.got_ref = bf16[16,32,512]{2,1,0:T(8,128)(2,1)S(1)} async-done(((bf16[16,32,512]{2,1,0:T(8,128)(2,1)}), bf16[16,32,512]{2,1,0:T(8,128)(2,1)S(1)}, u32[]{:S(2)}, u32[]{:S(2)}) %all-to-all-start) | async-done | bytes 524320 | tf_op jit(solution)/shard_map/all_to_all | solution.py:194
  46.6 0.0 copy-start
  46.6 2.1 %collective-permute-start.2 = (f32[8,2048]{1,0:T(8,128)S(1)}, f32[8,2048]{1,0:T(8,128)S(1)}, u32[]{:S(2)}, u32[]{:S(2)}) collective-permute-start(f32[8,2048]{1,0:T(8,128)S(1)} %join.1), channel_id=1, source_target_pairs={{0,1},{1,0},{2,3},{3,2},{4,5},{5,4},{6,7},{7,6},{8,9},{9,8},{10,11... | collective-permute-start | bytes 196616 | tf_op jit(solution)/shard_map/ppermute | solution.py:207
  48.7 0.0 collective-permute-done.other_hbm
  48.7 0.0 copy-done
  48.7 2.2 %up.1 = f32[512,2048]{1,0:T(8,128)S(1)} custom-call(bf16[16,32,512]{2,1,0:T(8,128)(2,1)S(1)} %all-to-all-done.got_ref, bf16[448,2048]{1,0:T(8,128)(2,1)S(1)} %bitcast.35, bf16[448,2048]{1,0:T(8,128)(2,1)} %collective-permute-done.other_hbm), custom_call_target="tpu_custom_call" | custom-call | tf_op jit(solution)/shard_map/up/pallas_call | solution.py:208
  50.9 0.0 collective-permute-done.2
  50.9 0.5 add_convert_fusion
  51.5 19.0 %all_to_all.15 = f16[4,128,2048]{2,1,0:T(8,128)(2,1)S(1)} all-to-all(f16[4,128,2048]{2,1,0:T(8,128)(2,1)S(1)} %bitcast.39), channel_id=1, replica_groups={{0,32,64,96},{128,160,192,224},{256,288,320,352},{384,416,448,480},{1,1..., dimensions={0} | all-to-all | bytes 4194304 | tf_op jit(solution)/shard_map/all_to_all | solution.py:222
  70.5 0.4 add_convert_fusion.1
  70.9 16.5 %all-gather.2 = f16[4,128,2048]{2,1,0:T(8,128)(2,1)S(1)} all-gather(f16[1,128,2048]{2,1,0:T(8,128)(2,1)S(1)} %add_convert_fusion.1), channel_id=1, replica_groups={{0,128,256,384},{32,160,288,416},{64,192,320,448},{96,224,352,480},{1,3..., dimensions={0}, use_global_device_ids=true | all-gather | bytes 2621440 | tf_op jit(solution)/shard_map/all_gather | solution.py:226
  87.4 0.6 multiply_convert_fusion.3
  87.9 0.0 copy-start.3
  87.9 16.1 %all-gather.3 = f16[512,2048]{1,0:T(8,128)(2,1)S(1)} all-gather(f16[128,2048]{1,0:T(8,128)(2,1)S(1)} %multiply_convert_fusion.3), channel_id=1, replica_groups={{0,32,64,96},{128,160,192,224},{256,288,320,352},{384,416,448,480},{1,1..., dimensions={0}, use_global_device_ids=true | all-gather | bytes 2621440 | tf_op jit(solution)/shard_map/all_gather | solution.py:230
  104.0 0.2 multiply_convert_fusion.active_ref
  104.3 0.0 copy-done.3
  104.3 0.7 fusion.2
  105.0 0.1 copy.9.own_ref
  105.1 0.0 copy-start.1
  105.1 0.0 copy-start.2
  105.1 0.8 down.1
  105.9 28.9 %all_to_all.16 = bf16[16,112,128]{2,1,0:T(8,128)(2,1)S(1)} all-to-all(bf16[16,112,128]{2,1,0:T(8,128)(2,1)S(1)} %bitcast.32), channel_id=1, replica_groups={{0,2,4,6,8,10,12,14,16,18,20,22,24,26,28,30},{1,3,5,7,9,11,13,15,17,19,..., dimensions={0} | all-to-all | bytes 917504 | tf_op jit(solution)/shard_map/all_to_all | solution.py:244
  134.8 0.0 copy-done.1
  134.8 0.0 copy-done.2
  134.8 1.3 combine.1
  (2 shorter events, 0.0 us)
Async XLA Ops:
  2.3 44.3 %all-to-all-start = ((bf16[16,32,512]{2,1,0:T(8,128)(2,1)}), bf16[16,32,512]{2,1,0:T(8,128)(2,1)S(1)}, u32[]{:S(2)}, u32[]{:S(2)}) async-start(bf16[16,32,512]{2,1,0:T(8,128)(2,1)} %bitcast.40), calls=%async_computation | async-start | bytes 1048576 | tf_op jit(solution)/shard_map/all_to_all | solution.py:194
  17.5 5.9 %collective-permute-start.1 = (bf16[448,2048]{1,0:T(8,128)(2,1)}, bf16[448,2048]{1,0:T(8,128)(2,1)S(1)}, u32[]{:S(2)}, u32[]{:S(2)}) collective-permute-start(bf16[448,2048]{1,0:T(8,128)(2,1)} %bitcast.43), channel_id=1, source_target_pairs={{0,1},{1,0},{2,3},{3,2},{4,5},{5,4},{6,7},{7,6},{8,9},{9,8},{10,11... | collective-permute-start | bytes 5505032 | tf_op jit(solution)/shard_map/ppermute | solution.py:193
  19.4 29.2 %collective-permute-start = (bf16[448,2048]{1,0:T(8,128)(2,1)}, bf16[448,2048]{1,0:T(8,128)(2,1)}, u32[]{:S(2)}, u32[]{:S(2)}) collective-permute-start(bf16[448,2048]{1,0:T(8,128)(2,1)} %bitcast.34), channel_id=1, source_target_pairs={{0,1},{1,0},{2,3},{3,2},{4,5},{5,4},{6,7},{7,6},{8,9},{9,8},{10,11... | collective-permute-start | bytes 5505032 | tf_op jit(solution)/shard_map/ppermute | solution.py:192
  46.6 2.1 %copy-start = (bf16[1,448,2048]{2,1,0:T(8,128)(2,1)S(1)}, bf16[1,448,2048]{2,1,0:T(8,128)(2,1)}, u32[]{:S(2)}) copy-start(bf16[1,448,2048]{2,1,0:T(8,128)(2,1)} %param.10) | copy-start | bytes 5505028
  46.6 4.3 %collective-permute-start.2 = (f32[8,2048]{1,0:T(8,128)S(1)}, f32[8,2048]{1,0:T(8,128)S(1)}, u32[]{:S(2)}, u32[]{:S(2)}) collective-permute-start(f32[8,2048]{1,0:T(8,128)S(1)} %join.1), channel_id=1, source_target_pairs={{0,1},{1,0},{2,3},{3,2},{4,5},{5,4},{6,7},{7,6},{8,9},{9,8},{10,11... | collective-permute-start | bytes 196616 | tf_op jit(solution)/shard_map/ppermute | solution.py:207
  87.9 16.3 %copy-start.3 = (bf16[1,2048,448]{1,2,0:T(8,128)(2,1)S(1)}, bf16[1,2048,448]{1,2,0:T(8,128)(2,1)}, u32[]{:S(2)}) copy-start(bf16[1,2048,448]{1,2,0:T(8,128)(2,1)} %param.11) | copy-start | bytes 5505028
  105.1 29.7 %copy-start.1 = (s32[256,8]{0,1:T(8,128)S(1)}, s32[256,8]{0,1:T(8,128)}, u32[]{:S(2)}) copy-start(s32[256,8]{0,1:T(8,128)} %param.8) | copy-start | bytes 24580
  105.1 29.7 %copy-start.2 = (bf16[256,8]{0,1:T(8,128)(2,1)S(1)}, bf16[256,8]{0,1:T(8,128)(2,1)}, u32[]{:S(2)}) copy-start(bf16[256,8]{0,1:T(8,128)(2,1)} %param.9) | copy-start | bytes 12292

commit v5 on v4

--- a/solution.py
+++ b/solution.py
@@ -64,7 +64,6 @@
     ]
     for copy in copies:
         copy.start()
-    width = rows_ref.shape[0]
     copies[0].wait()
     hits = jnp.where(slot_hits(relabel(routes_ref[...]), experts, capacity), 1.0, 0.0)
     copies[1].wait()
@@ -72,10 +71,24 @@
     scale = jnp.sum(hits * scale, axis=1, keepdims=True)
     copies[2].wait()
     picked = lax.dot_general(hits.astype(BF16), rows_ref[...], NT, preferred_element_type=F32)
-    out_ref[:, :width] = picked.astype(BF16)
-    out_ref[:, width:] = jnp.broadcast_to(
-        scale.astype(BF16), (out_ref.shape[0], out_ref.shape[1] - width)
-    )
+    width = rows_ref.shape[0]
+    whole = width // 128
+    half = capacity // 2
+    chunks = out_ref.shape[0]
+    picked = picked.reshape(chunks, 2, capacity, width)
+    tails = picked[..., whole * 128 :].reshape(chunks, 2, 2, half, width - whole * 128)
+    for i in range(2):
+        for j in range(whole):
+            at = (i * whole + j) * capacity
+            out_ref[:, at : at + capacity, :] = picked[:, i, :, j * 128 : (j + 1) * 128].astype(BF16)
+        at = 2 * whole * capacity + i * half
+        out_ref[:, at : at + half, :] = jnp.concatenate(
+            [tails[:, i, 0], tails[:, i, 1]], axis=-1
+        ).astype(BF16)
+    scale = jnp.broadcast_to(scale, (scale.shape[0], 32)).reshape(chunks, 4, half, 32)
+    out_ref[:, 2 * capacity * width // 128 :, :] = jnp.concatenate(
+        [scale[:, g] for g in range(4)], axis=-1
+    ).astype(BF16)
 
 
 def slot_gates(routes_t, gate_t, experts, capacity):
@@ -101,13 +114,26 @@
     copy = pltpu.make_async_copy(other_hbm, other_ref, sem)
     copy.start()
     width, hidden = own_ref.shape
-    slots = got_ref.shape[0] * capacity
+    chunks = got_ref.shape[0]
+    slots = chunks * capacity
+    whole = width // 128
+    half = capacity // 2
+    rest = width - whole * 128
+    scales = got_ref[:, 2 * capacity * width // 128 :, :].astype(F32)
     for i, weight_ref in enumerate((own_ref, other_ref)):
         if i == 1:
             copy.wait()
-        rows = got_ref[:, i * capacity : (i + 1) * capacity, :].reshape(slots, got_ref.shape[2])
-        scale = rows[:, width : width + 1].astype(F32) * WIRE_GAIN
-        rows = rows[:, :width]
+        columns = []
+        for j in range(whole):
+            at = (i * whole + j) * capacity
+            columns.append(got_ref[:, at : at + capacity, :].reshape(slots, 128))
+        at = 2 * whole * capacity + i * half
+        tail = got_ref[:, at : at + half, :].astype(F32)
+        tail = jnp.stack([tail[:, :, :rest], tail[:, :, rest:]], axis=1)
+        columns.append(tail.reshape(slots, rest).astype(BF16))
+        rows = jnp.concatenate(columns, axis=1)
+        scale = jnp.stack([scales[:, :, 64 * i : 64 * i + 1], scales[:, :, 64 * i + 32 : 64 * i + 33]], axis=1)
+        scale = scale.reshape(slots, 1) * WIRE_GAIN
         for j in range(0, hidden, TILE):
             term = jnp.dot(rows, weight_ref[:, j : j + TILE], preferred_element_type=F32)
             out_ref[i * slots : (i + 1) * slots, j : j + TILE] = term * scale
@@ -166,7 +192,8 @@
     hidden = up_weight.shape[2]
     capacity = tokens // 16
     slots = experts * capacity
-    padded = -(-(width + 1) // 128) * 128
+    chips = experts // 2
+    sent = 2 * capacity * width // 128 + capacity // 2
     params = pltpu.CompilerParams(vmem_limit_bytes=VMEM_LIMIT)
     rows_t = token_rows.T
     routes_t = routes.T
@@ -174,7 +201,7 @@
 
     send = pl.pallas_call(
         functools.partial(pick_kernel, experts, capacity),
-        out_shape=jax.ShapeDtypeStruct((slots, padded), BF16),
+        out_shape=jax.ShapeDtypeStruct((chips, sent, 128), BF16),
         in_specs=[pl.BlockSpec(memory_space=pltpu.HBM)] * 3,
         out_specs=vmem_spec(),
         scratch_shapes=[
@@ -185,15 +212,13 @@
         ],
         name="pick",
     )(rows_t, row_scale, routes_t)
-    chips = experts // 2
     rings = [[2 * chip + core for chip in range(chips)] for core in range(2)]
     swap = [(i, i ^ 1) for i in range(experts)]
     up_own, down_own = up_weight[0], down_weight[0].T
     up_other = lax.ppermute(up_own, "expert", swap)
     down_other = lax.ppermute(down_own, "expert", swap)
     got = lax.all_to_all(
-        send.reshape(chips, 2 * capacity, padded), "expert", 0, 0, tiled=True,
-        axis_index_groups=rings,
+        send, "expert", 0, 0, tiled=True, axis_index_groups=rings
     )
     anywhere = pl.BlockSpec(memory_space=pl.ANY)
     after = pl.pallas_call(

time: 137 us -> 135 us (0.985)
  no operation moved by 1% of the time
where the time goes in v5:
time: 135 us
  blocking collectives  80 us (59%)
  waiting for transfers between devices  23.8 us (18%)
  starting transfers between devices  21.6 us (16%)
  Pallas kernels  6.63 us (5%)
  other arithmetic  1.75 us (1%)
    all_to_all x1, blocking collectives, on_device(): lax.all_to_all(pieces.reshape(chips, 2 * packed, 128), 'expert', 0, 0, ti...  28.4 us
    all_to_all x1, waiting for transfers between devices, on_device(): lax.all_to_all(send, 'expert', 0, 0, tiled=True, axis_index_groups=rings)  22.3 us
    all_to_all x1, blocking collectives, on_device(): lax.all_to_all(terms.reshape(side, side_slots, hidden), plane, 0, 0, tile...  19 us
    all_gather x1, blocking collectives, on_device(): partial = lax.all_gather(partial, plane, axis=0, axis_index_groups=second)  16.5 us
    all_gather x1, blocking collectives, on_device(): lax.all_gather(active, plane, axis=0, tiled=True, axis_index_groups=first)  16.1 us
    all_to_all x1, starting transfers between devices, on_device(): lax.all_to_all(send, 'expert', 0, 0, tiled=True, axis_index_groups=rings)  15.2 us
  transfers between devices with their start and end apart: 4, of which 2 were waited for; matrix products, arithmetic and copies ran while one was open for 0% of the time, Pallas kernels for 2%

profile of v5, /device:TPU:6, one launch (start us, length us, event | category | flops | bytes accessed | tf_op | source)
XLA Modules:
  0.0 134.7 jit_solution(3358218707321884102)
XLA Ops:
  0.0 2.3 %pick.1 = bf16[16,120,128]{2,1,0:T(8,128)(2,1)} custom-call(bf16[448,256]{1,0:T(8,128)(2,1)} %bitcast.39, bf16[256]{0:T(256)(128)(2,1)} %scale_hbm.1, s32[8,256]{1,0:T(8,128)} %bitcast.35), custom_call_target="tpu_custom_call" | custom-call | tf_op jit(solution)/shard_map/pick/pallas_call | solution.py:202
  2.4 15.2 %all-to-all-start = ((bf16[16,120,128]{2,1,0:T(8,128)(2,1)}), bf16[16,120,128]{2,1,0:T(8,128)(2,1)S(1)}, u32[]{:S(2)}, u32[]{:S(2)}) async-start(bf16[16,120,128]{2,1,0:T(8,128)(2,1)} %pick.1), calls=%async_computation | async-start | bytes 983040 | tf_op jit(solution)/shard_map/all_to_all | solution.py:220
  17.6 1.9 %collective-permute-start.1 = (bf16[448,2048]{1,0:T(8,128)(2,1)}, bf16[448,2048]{1,0:T(8,128)(2,1)S(1)}, u32[]{:S(2)}, u32[]{:S(2)}) collective-permute-start(bf16[448,2048]{1,0:T(8,128)(2,1)} %bitcast.41), channel_id=1, source_target_pairs={{0,1},{1,0},{2,3},{3,2},{4,5},{5,4},{6,7},{7,6},{8,9},{9,8},{10,11... | collective-permute-start | bytes 5505032 | tf_op jit(solution)/shard_map/ppermute | solution.py:219
  19.5 2.4 %collective-permute-start = (bf16[448,2048]{1,0:T(8,128)(2,1)}, bf16[448,2048]{1,0:T(8,128)(2,1)}, u32[]{:S(2)}, u32[]{:S(2)}) collective-permute-start(bf16[448,2048]{1,0:T(8,128)(2,1)} %bitcast.33), channel_id=1, source_target_pairs={{0,1},{1,0},{2,3},{3,2},{4,5},{5,4},{6,7},{7,6},{8,9},{9,8},{10,11... | collective-permute-start | bytes 5505032 | tf_op jit(solution)/shard_map/ppermute | solution.py:218
  21.9 1.5 %collective-permute-done.1.later_ref.weight_ref = bf16[448,2048]{1,0:T(8,128)(2,1)S(1)} collective-permute-done((bf16[448,2048]{1,0:T(8,128)(2,1)}, bf16[448,2048]{1,0:T(8,128)(2,1)S(1)}, u32[]{:S(2)}, u32[]{:S(2)}) %collective-permute-start.1) | collective-permute-done | bytes 1835040 | tf_op jit(solution)/shard_map/ppermute | solution.py:219
  23.5 22.3 %all-to-all-done.got_ref = bf16[16,120,128]{2,1,0:T(8,128)(2,1)S(1)} async-done(((bf16[16,120,128]{2,1,0:T(8,128)(2,1)}), bf16[16,120,128]{2,1,0:T(8,128)(2,1)S(1)}, u32[]{:S(2)}, u32[]{:S(2)}) %all-to-all-start) | async-done | bytes 491552 | tf_op jit(solution)/shard_map/all_to_all | solution.py:220
  45.7 0.0 copy-start
  45.7 2.1 %collective-permute-start.2 = (f32[8,2048]{1,0:T(8,128)S(1)}, f32[8,2048]{1,0:T(8,128)S(1)}, u32[]{:S(2)}, u32[]{:S(2)}) collective-permute-start(f32[8,2048]{1,0:T(8,128)S(1)} %join.1), channel_id=1, source_target_pairs={{0,1},{1,0},{2,3},{3,2},{4,5},{5,4},{6,7},{7,6},{8,9},{9,8},{10,11... | collective-permute-start | bytes 196616 | tf_op jit(solution)/shard_map/ppermute | solution.py:232
  47.8 0.0 collective-permute-done.other_hbm
  47.8 0.0 copy-done
  47.8 2.2 %up.1 = f32[512,2048]{1,0:T(8,128)S(1)} custom-call(bf16[16,120,128]{2,1,0:T(8,128)(2,1)S(1)} %all-to-all-done.got_ref, bf16[448,2048]{1,0:T(8,128)(2,1)S(1)} %bitcast.34, bf16[448,2048]{1,0:T(8,128)(2,1)} %collective-permute-done.other_hbm), custom_call_target="tpu_custom_call" | custom-call | tf_op jit(solution)/shard_map/up/pallas_call | solution.py:233
  50.0 0.0 collective-permute-done.2
  50.1 0.5 add_convert_fusion
  50.6 19.0 %all_to_all.15 = f16[4,128,2048]{2,1,0:T(8,128)(2,1)S(1)} all-to-all(f16[4,128,2048]{2,1,0:T(8,128)(2,1)S(1)} %bitcast.38), channel_id=1, replica_groups={{0,32,64,96},{128,160,192,224},{256,288,320,352},{384,416,448,480},{1,1..., dimensions={0} | all-to-all | bytes 4194304 | tf_op jit(solution)/shard_map/all_to_all | solution.py:247
  69.6 0.4 add_convert_fusion.1
  70.0 16.5 %all-gather.2 = f16[4,128,2048]{2,1,0:T(8,128)(2,1)S(1)} all-gather(f16[1,128,2048]{2,1,0:T(8,128)(2,1)S(1)} %add_convert_fusion.1), channel_id=1, replica_groups={{0,128,256,384},{32,160,288,416},{64,192,320,448},{96,224,352,480},{1,3..., dimensions={0}, use_global_device_ids=true | all-gather | bytes 2621440 | tf_op jit(solution)/shard_map/all_gather | solution.py:251
  86.5 0.6 multiply_convert_fusion.3
  87.1 0.0 copy-start.3
  87.1 16.1 %all-gather.3 = f16[512,2048]{1,0:T(8,128)(2,1)S(1)} all-gather(f16[128,2048]{1,0:T(8,128)(2,1)S(1)} %multiply_convert_fusion.3), channel_id=1, replica_groups={{0,32,64,96},{128,160,192,224},{256,288,320,352},{384,416,448,480},{1,1..., dimensions={0}, use_global_device_ids=true | all-gather | bytes 2621440 | tf_op jit(solution)/shard_map/all_gather | solution.py:255
  103.2 0.2 multiply_convert_fusion.active_ref
  103.4 0.0 copy-done.3
  103.4 0.7 fusion.2
  104.1 0.1 copy.9.own_ref
  104.2 0.0 copy-start.1
  104.3 0.0 copy-start.2
  104.3 0.8 down.1
  105.1 28.4 %all_to_all.16 = bf16[16,112,128]{2,1,0:T(8,128)(2,1)S(1)} all-to-all(bf16[16,112,128]{2,1,0:T(8,128)(2,1)S(1)} %bitcast.31), channel_id=1, replica_groups={{0,2,4,6,8,10,12,14,16,18,20,22,24,26,28,30},{1,3,5,7,9,11,13,15,17,19,..., dimensions={0} | all-to-all | bytes 917504 | tf_op jit(solution)/shard_map/all_to_all | solution.py:269
  133.5 0.0 copy-done.1
  133.5 0.0 copy-done.2
  133.5 1.3 combine.1
  (2 shorter events, 0.0 us)
Async XLA Ops:
  2.4 43.4 %all-to-all-start = ((bf16[16,120,128]{2,1,0:T(8,128)(2,1)}), bf16[16,120,128]{2,1,0:T(8,128)(2,1)S(1)}, u32[]{:S(2)}, u32[]{:S(2)}) async-start(bf16[16,120,128]{2,1,0:T(8,128)(2,1)} %pick.1), calls=%async_computation | async-start | bytes 983040 | tf_op jit(solution)/shard_map/all_to_all | solution.py:220
  17.6 5.9 %collective-permute-start.1 = (bf16[448,2048]{1,0:T(8,128)(2,1)}, bf16[448,2048]{1,0:T(8,128)(2,1)S(1)}, u32[]{:S(2)}, u32[]{:S(2)}) collective-permute-start(bf16[448,2048]{1,0:T(8,128)(2,1)} %bitcast.41), channel_id=1, source_target_pairs={{0,1},{1,0},{2,3},{3,2},{4,5},{5,4},{6,7},{7,6},{8,9},{9,8},{10,11... | collective-permute-start | bytes 5505032 | tf_op jit(solution)/shard_map/ppermute | solution.py:219
  19.5 28.3 %collective-permute-start = (bf16[448,2048]{1,0:T(8,128)(2,1)}, bf16[448,2048]{1,0:T(8,128)(2,1)}, u32[]{:S(2)}, u32[]{:S(2)}) collective-permute-start(bf16[448,2048]{1,0:T(8,128)(2,1)} %bitcast.33), channel_id=1, source_target_pairs={{0,1},{1,0},{2,3},{3,2},{4,5},{5,4},{6,7},{7,6},{8,9},{9,8},{10,11... | collective-permute-start | bytes 5505032 | tf_op jit(solution)/shard_map/ppermute | solution.py:218
  45.7 2.1 %copy-start = (bf16[1,448,2048]{2,1,0:T(8,128)(2,1)S(1)}, bf16[1,448,2048]{2,1,0:T(8,128)(2,1)}, u32[]{:S(2)}) copy-start(bf16[1,448,2048]{2,1,0:T(8,128)(2,1)} %param.10) | copy-start | bytes 5505028
  45.7 4.3 %collective-permute-start.2 = (f32[8,2048]{1,0:T(8,128)S(1)}, f32[8,2048]{1,0:T(8,128)S(1)}, u32[]{:S(2)}, u32[]{:S(2)}) collective-permute-start(f32[8,2048]{1,0:T(8,128)S(1)} %join.1), channel_id=1, source_target_pairs={{0,1},{1,0},{2,3},{3,2},{4,5},{5,4},{6,7},{7,6},{8,9},{9,8},{10,11... | collective-permute-start | bytes 196616 | tf_op jit(solution)/shard_map/ppermute | solution.py:232
  87.1 16.3 %copy-start.3 = (bf16[1,2048,448]{1,2,0:T(8,128)(2,1)S(1)}, bf16[1,2048,448]{1,2,0:T(8,128)(2,1)}, u32[]{:S(2)}) copy-start(bf16[1,2048,448]{1,2,0:T(8,128)(2,1)} %param.11) | copy-start | bytes 5505028
  104.2 29.2 %copy-start.1 = (s32[256,8]{0,1:T(8,128)S(1)}, s32[256,8]{0,1:T(8,128)}, u32[]{:S(2)}) copy-start(s32[256,8]{0,1:T(8,128)} %param.8) | copy-start | bytes 24580
  104.3 29.2 %copy-start.2 = (bf16[256,8]{0,1:T(8,128)(2,1)S(1)}, bf16[256,8]{0,1:T(8,128)(2,1)}, u32[]{:S(2)}) copy-start(bf16[256,8]{0,1:T(8,128)(2,1)} %param.9) | copy-start | bytes 12292

commit v6 on v5

--- a/solution.py
+++ b/solution.py
@@ -229,7 +229,7 @@
         compiler_params=params,
         name="join",
     )(got, down_other)
-    after = lax.ppermute(after, "expert", swap)
+    after = lax.ppermute(after, "expert", [(i, i + 1) for i in range(0, experts, 2)])
     terms = pl.pallas_call(
         functools.partial(up_kernel, capacity),
         out_shape=jax.ShapeDtypeStruct((slots, hidden), F32),
@@ -241,7 +241,7 @@
     )(got, up_own, up_other)
     terms = (terms + after[:1]).astype(WIRE)
     plane = ("pipe", "expert")
-    first, second = plane_groups(shares, experts, True), plane_groups(shares, experts, False)
+    first, second = plane_groups(shares, experts, False), plane_groups(shares, experts, True)
     side = len(first[0])
     side_slots = slots // side
     parts = lax.all_to_all(

time: 135 us -> 134 us (level); the launches traced: 135 us -> 132 us
  blocking collectives: 80 us -> 77.9 us
    all_to_all x1, blocking collectives: 28.4 us -> 25.1 us  [on_device(): lax.all_to_all(pieces.reshape(chips, 2 * packed, 128), 'expert', 0, 0, ti...]
    all_to_all x1, blocking collectives: 19 us -> 20.8 us  [on_device(): lax.all_to_all(terms.reshape(side, side_slots, hidden), plane, 0, 0, tile...]
where the time goes in v6:
time: 134 us; the launch traced here: 132 us
  blocking collectives  77.9 us (58%)
  waiting for transfers between devices  23.8 us (18%)
  starting transfers between devices  21 us (16%)
  Pallas kernels  6.63 us (5%)
  other arithmetic  1.75 us (1%)
    all_to_all x1, blocking collectives, on_device(): lax.all_to_all(pieces.reshape(chips, 2 * packed, 128), 'expert', 0, 0, ti...  25.1 us
    all_to_all x1, waiting for transfers between devices, on_device(): lax.all_to_all(send, 'expert', 0, 0, tiled=True, axis_index_groups=rings)  22.3 us
    all_to_all x1, blocking collectives, on_device(): lax.all_to_all(terms.reshape(side, side_slots, hidden), plane, 0, 0, tile...  20.8 us
    all_gather x1, blocking collectives, on_device(): lax.all_gather(active, plane, axis=0, tiled=True, axis_index_groups=first)  16.1 us
    all_gather x1, blocking collectives, on_device(): partial = lax.all_gather(partial, plane, axis=0, axis_index_groups=second)  15.9 us
    all_to_all x1, starting transfers between devices, on_device(): lax.all_to_all(send, 'expert', 0, 0, tiled=True, axis_index_groups=rings)  15.2 us
  transfers between devices with their start and end apart: 4, of which 2 were waited for; matrix products, arithmetic and copies ran while one was open for 0% of the time, Pallas kernels for 2%

profile of v6, /device:TPU:6, one launch (start us, length us, event | category | flops | bytes accessed | tf_op | source)
XLA Modules:
  0.0 132.1 jit_solution(7073456999052416613)
XLA Ops:
  0.0 2.3 %pick.1 = bf16[16,120,128]{2,1,0:T(8,128)(2,1)} custom-call(bf16[448,256]{1,0:T(8,128)(2,1)} %bitcast.39, bf16[256]{0:T(256)(128)(2,1)} %scale_hbm.1, s32[8,256]{1,0:T(8,128)} %bitcast.35), custom_call_target="tpu_custom_call" | custom-call | tf_op jit(solution)/shard_map/pick/pallas_call | solution.py:202
  2.4 15.2 %all-to-all-start = ((bf16[16,120,128]{2,1,0:T(8,128)(2,1)}), bf16[16,120,128]{2,1,0:T(8,128)(2,1)S(1)}, u32[]{:S(2)}, u32[]{:S(2)}) async-start(bf16[16,120,128]{2,1,0:T(8,128)(2,1)} %pick.1), calls=%async_computation | async-start | bytes 983040 | tf_op jit(solution)/shard_map/all_to_all | solution.py:220
  17.6 1.9 %collective-permute-start.1 = (bf16[448,2048]{1,0:T(8,128)(2,1)}, bf16[448,2048]{1,0:T(8,128)(2,1)S(1)}, u32[]{:S(2)}, u32[]{:S(2)}) collective-permute-start(bf16[448,2048]{1,0:T(8,128)(2,1)} %bitcast.41), channel_id=1, source_target_pairs={{0,1},{1,0},{2,3},{3,2},{4,5},{5,4},{6,7},{7,6},{8,9},{9,8},{10,11... | collective-permute-start | bytes 5505032 | tf_op jit(solution)/shard_map/ppermute | solution.py:219
  19.5 2.4 %collective-permute-start = (bf16[448,2048]{1,0:T(8,128)(2,1)}, bf16[448,2048]{1,0:T(8,128)(2,1)}, u32[]{:S(2)}, u32[]{:S(2)}) collective-permute-start(bf16[448,2048]{1,0:T(8,128)(2,1)} %bitcast.33), channel_id=1, source_target_pairs={{0,1},{1,0},{2,3},{3,2},{4,5},{5,4},{6,7},{7,6},{8,9},{9,8},{10,11... | collective-permute-start | bytes 5505032 | tf_op jit(solution)/shard_map/ppermute | solution.py:218
  21.9 1.5 %collective-permute-done.1.later_ref.weight_ref = bf16[448,2048]{1,0:T(8,128)(2,1)S(1)} collective-permute-done((bf16[448,2048]{1,0:T(8,128)(2,1)}, bf16[448,2048]{1,0:T(8,128)(2,1)S(1)}, u32[]{:S(2)}, u32[]{:S(2)}) %collective-permute-start.1) | collective-permute-done | bytes 1835040 | tf_op jit(solution)/shard_map/ppermute | solution.py:219
  23.5 22.3 %all-to-all-done.got_ref = bf16[16,120,128]{2,1,0:T(8,128)(2,1)S(1)} async-done(((bf16[16,120,128]{2,1,0:T(8,128)(2,1)}), bf16[16,120,128]{2,1,0:T(8,128)(2,1)S(1)}, u32[]{:S(2)}, u32[]{:S(2)}) %all-to-all-start) | async-done | bytes 491552 | tf_op jit(solution)/shard_map/all_to_all | solution.py:220
  45.7 0.0 copy-start
  45.7 1.4 %collective-permute-start.2 = (f32[8,2048]{1,0:T(8,128)S(1)}, f32[8,2048]{1,0:T(8,128)S(1)}, u32[]{:S(2)}, u32[]{:S(2)}) collective-permute-start(f32[8,2048]{1,0:T(8,128)S(1)} %join.1), channel_id=1, source_target_pairs={{0,1},{2,3},{4,5},{6,7},{8,9},{10,11},{12,13},{14,15},{16,17},{18,... | collective-permute-start | bytes 196616 | tf_op jit(solution)/shard_map/ppermute | solution.py:232
  47.2 0.0 collective-permute-done.other_hbm
  47.2 0.0 copy-done
  47.2 2.2 %up.1 = f32[512,2048]{1,0:T(8,128)S(1)} custom-call(bf16[16,120,128]{2,1,0:T(8,128)(2,1)S(1)} %all-to-all-done.got_ref, bf16[448,2048]{1,0:T(8,128)(2,1)S(1)} %bitcast.34, bf16[448,2048]{1,0:T(8,128)(2,1)} %collective-permute-done.other_hbm), custom_call_target="tpu_custom_call" | custom-call | tf_op jit(solution)/shard_map/up/pallas_call | solution.py:233
  49.5 0.0 collective-permute-done.2
  49.5 0.5 add_convert_fusion
  50.0 20.8 %all_to_all.15 = f16[4,128,2048]{2,1,0:T(8,128)(2,1)S(1)} all-to-all(f16[4,128,2048]{2,1,0:T(8,128)(2,1)S(1)} %bitcast.38), channel_id=1, replica_groups={{0,128,256,384},{32,160,288,416},{64,192,320,448},{96,224,352,480},{1,3..., dimensions={0} | all-to-all | bytes 4194304 | tf_op jit(solution)/shard_map/all_to_all | solution.py:247
  70.8 0.4 add_convert_fusion.1
  71.2 15.9 %all-gather.2 = f16[4,128,2048]{2,1,0:T(8,128)(2,1)S(1)} all-gather(f16[1,128,2048]{2,1,0:T(8,128)(2,1)S(1)} %add_convert_fusion.1), channel_id=1, replica_groups={{0,32,64,96},{128,160,192,224},{256,288,320,352},{384,416,448,480},{1,1..., dimensions={0}, use_global_device_ids=true | all-gather | bytes 2621440 | tf_op jit(solution)/shard_map/all_gather | solution.py:251
  87.1 0.6 multiply_convert_fusion.3
  87.7 0.0 copy-start.3
  87.7 16.1 %all-gather.3 = f16[512,2048]{1,0:T(8,128)(2,1)S(1)} all-gather(f16[128,2048]{1,0:T(8,128)(2,1)S(1)} %multiply_convert_fusion.3), channel_id=1, replica_groups={{0,128,256,384},{32,160,288,416},{64,192,320,448},{96,224,352,480},{1,3..., dimensions={0}, use_global_device_ids=true | all-gather | bytes 2621440 | tf_op jit(solution)/shard_map/all_gather | solution.py:255
  103.8 0.2 multiply_convert_fusion.active_ref
  104.1 0.0 copy-done.3
  104.1 0.7 fusion.2
  104.8 0.1 copy.9.own_ref
  104.9 0.0 copy-start.1
  104.9 0.0 copy-start.2
  104.9 0.8 down.1
  105.7 25.1 %all_to_all.16 = bf16[16,112,128]{2,1,0:T(8,128)(2,1)S(1)} all-to-all(bf16[16,112,128]{2,1,0:T(8,128)(2,1)S(1)} %bitcast.31), channel_id=1, replica_groups={{0,2,4,6,8,10,12,14,16,18,20,22,24,26,28,30},{1,3,5,7,9,11,13,15,17,19,..., dimensions={0} | all-to-all | bytes 917504 | tf_op jit(solution)/shard_map/all_to_all | solution.py:269
  130.8 0.0 copy-done.1
  130.8 0.0 copy-done.2
  130.8 1.3 combine.1
  (2 shorter events, 0.0 us)
Async XLA Ops:
  2.4 43.4 %all-to-all-start = ((bf16[16,120,128]{2,1,0:T(8,128)(2,1)}), bf16[16,120,128]{2,1,0:T(8,128)(2,1)S(1)}, u32[]{:S(2)}, u32[]{:S(2)}) async-start(bf16[16,120,128]{2,1,0:T(8,128)(2,1)} %pick.1), calls=%async_computation | async-start | bytes 983040 | tf_op jit(solution)/shard_map/all_to_all | solution.py:220
  17.6 5.9 %collective-permute-start.1 = (bf16[448,2048]{1,0:T(8,128)(2,1)}, bf16[448,2048]{1,0:T(8,128)(2,1)S(1)}, u32[]{:S(2)}, u32[]{:S(2)}) collective-permute-start(bf16[448,2048]{1,0:T(8,128)(2,1)} %bitcast.41), channel_id=1, source_target_pairs={{0,1},{1,0},{2,3},{3,2},{4,5},{5,4},{6,7},{7,6},{8,9},{9,8},{10,11... | collective-permute-start | bytes 5505032 | tf_op jit(solution)/shard_map/ppermute | solution.py:219
  19.5 27.7 %collective-permute-start = (bf16[448,2048]{1,0:T(8,128)(2,1)}, bf16[448,2048]{1,0:T(8,128)(2,1)}, u32[]{:S(2)}, u32[]{:S(2)}) collective-permute-start(bf16[448,2048]{1,0:T(8,128)(2,1)} %bitcast.33), channel_id=1, source_target_pairs={{0,1},{1,0},{2,3},{3,2},{4,5},{5,4},{6,7},{7,6},{8,9},{9,8},{10,11... | collective-permute-start | bytes 5505032 | tf_op jit(solution)/shard_map/ppermute | solution.py:218
  45.7 1.5 %copy-start = (bf16[1,448,2048]{2,1,0:T(8,128)(2,1)S(1)}, bf16[1,448,2048]{2,1,0:T(8,128)(2,1)}, u32[]{:S(2)}) copy-start(bf16[1,448,2048]{2,1,0:T(8,128)(2,1)} %param.10) | copy-start | bytes 5505028
  45.7 3.7 %collective-permute-start.2 = (f32[8,2048]{1,0:T(8,128)S(1)}, f32[8,2048]{1,0:T(8,128)S(1)}, u32[]{:S(2)}, u32[]{:S(2)}) collective-permute-start(f32[8,2048]{1,0:T(8,128)S(1)} %join.1), channel_id=1, source_target_pairs={{0,1},{2,3},{4,5},{6,7},{8,9},{10,11},{12,13},{14,15},{16,17},{18,... | collective-permute-start | bytes 196616 | tf_op jit(solution)/shard_map/ppermute | solution.py:232
  87.7 16.3 %copy-start.3 = (bf16[1,2048,448]{1,2,0:T(8,128)(2,1)S(1)}, bf16[1,2048,448]{1,2,0:T(8,128)(2,1)}, u32[]{:S(2)}) copy-start(bf16[1,2048,448]{1,2,0:T(8,128)(2,1)} %param.11) | copy-start | bytes 5505028
  104.9 25.9 %copy-start.1 = (s32[256,8]{0,1:T(8,128)S(1)}, s32[256,8]{0,1:T(8,128)}, u32[]{:S(2)}) copy-start(s32[256,8]{0,1:T(8,128)} %param.8) | copy-start | bytes 24580
  104.9 25.9 %copy-start.2 = (bf16[256,8]{0,1:T(8,128)(2,1)S(1)}, bf16[256,8]{0,1:T(8,128)(2,1)}, u32[]{:S(2)}) copy-start(bf16[256,8]{0,1:T(8,128)(2,1)} %param.9) | copy-start | bytes 12292

commit v7 on v6

--- a/solution.py
+++ b/solution.py
@@ -81,10 +81,9 @@
         for j in range(whole):
             at = (i * whole + j) * capacity
             out_ref[:, at : at + capacity, :] = picked[:, i, :, j * 128 : (j + 1) * 128].astype(BF16)
-        at = 2 * whole * capacity + i * half
-        out_ref[:, at : at + half, :] = jnp.concatenate(
-            [tails[:, i, 0], tails[:, i, 1]], axis=-1
-        ).astype(BF16)
+    tails = jnp.concatenate([tails[:, :, 0], tails[:, :, 1]], axis=-1)
+    at = 2 * whole * capacity
+    out_ref[:, at : at + capacity, :] = tails.reshape(chunks, capacity, 128).astype(BF16)
     scale = jnp.broadcast_to(scale, (scale.shape[0], 32)).reshape(chunks, 4, half, 32)
     out_ref[:, 2 * capacity * width // 128 :, :] = jnp.concatenate(
         [scale[:, g] for g in range(4)], axis=-1
@@ -119,7 +118,9 @@
     whole = width // 128
     half = capacity // 2
     rest = width - whole * 128
-    scales = got_ref[:, 2 * capacity * width // 128 :, :].astype(F32)
+    at = 2 * whole * capacity
+    tails = got_ref[:, at : at + capacity, :].astype(F32)
+    scales = got_ref[:, at + capacity :, :].astype(F32)
     for i, weight_ref in enumerate((own_ref, other_ref)):
         if i == 1:
             copy.wait()
@@ -127,8 +128,7 @@
         for j in range(whole):
             at = (i * whole + j) * capacity
             columns.append(got_ref[:, at : at + capacity, :].reshape(slots, 128))
-        at = 2 * whole * capacity + i * half
-        tail = got_ref[:, at : at + half, :].astype(F32)
+        tail = tails[:, i * half : (i + 1) * half, :]
         tail = jnp.stack([tail[:, :, :rest], tail[:, :, rest:]], axis=1)
         columns.append(tail.reshape(slots, rest).astype(BF16))
         rows = jnp.concatenate(columns, axis=1)
@@ -146,15 +146,16 @@
     rest = width - whole * 128
     chunks = out_ref.shape[0]
     other = lax.dot_general(active_ref[...], weight_ref[...], NT, preferred_element_type=F32)
+    tails = []
     for i, piece in enumerate((own_ref[...].astype(F32), other)):
         for j in range(whole):
-            out_ref[:, i, j * capacity : (j + 1) * capacity, :] = (
+            at = (i * whole + j) * capacity
+            out_ref[:, at : at + capacity, :] = (
                 piece[:, j * 128 : (j + 1) * 128].astype(BF16).reshape(chunks, capacity, 128)
             )
         tail = piece[:, whole * 128 :].reshape(chunks, 2, half, rest)
-        out_ref[:, i, whole * capacity :, :] = jnp.concatenate(
-            [tail[:, 0], tail[:, 1]], axis=-1
-        ).astype(BF16)
+        tails.append(jnp.concatenate([tail[:, 0], tail[:, 1]], axis=-1))
+    out_ref[:, 2 * whole * capacity :, :] = jnp.concatenate(tails, axis=1).astype(BF16)
 
 
 def combine_kernel(capacity, width, back_ref, routes_ref, gate_ref, out_ref):
@@ -162,16 +163,23 @@
     whole = width // 128
     half = capacity // 2
     rest = width - whole * 128
-    gate = slot_gates(relabel(routes_ref[...]), gate_ref[...], chunks, capacity)
+    slots = chunks * 2 * capacity
+    gate = slot_gates(relabel(routes_ref[...]), gate_ref[...], chunks * 2, capacity)
     for j in range(whole):
-        column = back_ref[:, j * capacity : (j + 1) * capacity, :].reshape(chunks * capacity, 128)
+        column = jnp.stack(
+            [
+                back_ref[:, at : at + capacity, :]
+                for at in (j * capacity, (whole + j) * capacity)
+            ],
+            axis=1,
+        )
         out_ref[j * 128 : (j + 1) * 128, :] = lax.dot_general(
-            column, gate, TN, preferred_element_type=F32
+            column.reshape(slots, 128), gate, TN, preferred_element_type=F32
         )
-    tail = back_ref[:, whole * capacity :, :].astype(F32)
-    tail = jnp.stack([tail[:, :, :rest], tail[:, :, rest:]], axis=1)
-    tail = tail.reshape(chunks * capacity, rest).astype(BF16)
-    out_ref[whole * 128 :, :] = lax.dot_general(tail, gate, TN, preferred_element_type=F32)
+    tails = back_ref[:, 2 * whole * capacity :, :].astype(F32).reshape(chunks, 2, half, 128)
+    tails = jnp.stack([tails[..., :rest], tails[..., rest:]], axis=2)
+    tails = tails.reshape(slots, rest).astype(BF16)
+    out_ref[whole * 128 :, :] = lax.dot_general(tails, gate, TN, preferred_element_type=F32)
 
 
 def plane_groups(shares, experts, even_along_x):
@@ -257,18 +265,15 @@
         (rows.astype(F32) * (1.0 / ACTIVE_GAIN)).astype(BF16) for rows in jnp.split(active, 2)
     )
     own = lax.dot_general(own, down_own, NT, preferred_element_type=F32).astype(BF16)
-    packed = capacity * width // 128
     pieces = pl.pallas_call(
         functools.partial(down_kernel, capacity),
-        out_shape=jax.ShapeDtypeStruct((chips, 2, packed, 128), BF16),
+        out_shape=jax.ShapeDtypeStruct((chips, 2 * capacity * width // 128, 128), BF16),
         in_specs=[vmem_spec()] * 3,
         out_specs=vmem_spec(),
         compiler_params=params,
         name="down",
     )(own, other, down_other)
-    back = lax.all_to_all(
-        pieces.reshape(chips, 2 * packed, 128), "expert", 0, 0, tiled=True, axis_index_groups=rings
-    ).reshape(experts, packed, 128)
+    back = lax.all_to_all(pieces, "expert", 0, 0, tiled=True, axis_index_groups=rings)
     combined_t = pl.pallas_call(
         functools.partial(combine_kernel, capacity, width),
         out_shape=jax.ShapeDtypeStruct((width, tokens), F32),

time: 134 us -> 134 us (level)
  no operation moved by 1% of the time
where the time goes in v7:
time: 134 us; the launch traced here: 132 us
  blocking collectives  77.9 us (58%)
  waiting for transfers between devices  23.8 us (18%)
  starting transfers between devices  21 us (16%)
  Pallas kernels  6.63 us (5%)
  other arithmetic  1.75 us (1%)
    all_to_all x1, blocking collectives, on_device(): lax.all_to_all(pieces, 'expert', 0, 0, tiled=True, axis_index_groups=rings)  25.1 us
    all_to_all x1, waiting for transfers between devices, on_device(): lax.all_to_all(send, 'expert', 0, 0, tiled=True, axis_index_groups=rings)  22.3 us
    all_to_all x1, blocking collectives, on_device(): lax.all_to_all(terms.reshape(side, side_slots, hidden), plane, 0, 0, tile...  20.8 us
    all_gather x1, blocking collectives, on_device(): lax.all_gather(active, plane, axis=0, tiled=True, axis_index_groups=first)  16.1 us
    all_gather x1, blocking collectives, on_device(): partial = lax.all_gather(partial, plane, axis=0, axis_index_groups=second)  15.9 us
    all_to_all x1, starting transfers between devices, on_device(): lax.all_to_all(send, 'expert', 0, 0, tiled=True, axis_index_groups=rings)  15.2 us
  transfers between devices with their start and end apart: 4, of which 2 were waited for; matrix products, arithmetic and copies ran while one was open for 0% of the time, Pallas kernels for 2%

profile of v7, /device:TPU:6, one launch (start us, length us, event | category | flops | bytes accessed | tf_op | source)
XLA Modules:
  0.0 132.1 jit_solution(2128957955739578455)
XLA Ops:
  0.0 2.3 %pick.1 = bf16[16,120,128]{2,1,0:T(8,128)(2,1)} custom-call(bf16[448,256]{1,0:T(8,128)(2,1)} %bitcast.35, bf16[256]{0:T(256)(128)(2,1)} %scale_hbm.1, s32[8,256]{1,0:T(8,128)} %bitcast.31), custom_call_target="tpu_custom_call" | custom-call | tf_op jit(solution)/shard_map/pick/pallas_call | solution.py:210
  2.4 15.2 %all-to-all-start = ((bf16[16,120,128]{2,1,0:T(8,128)(2,1)}), bf16[16,120,128]{2,1,0:T(8,128)(2,1)S(1)}, u32[]{:S(2)}, u32[]{:S(2)}) async-start(bf16[16,120,128]{2,1,0:T(8,128)(2,1)} %pick.1), calls=%async_computation | async-start | bytes 983040 | tf_op jit(solution)/shard_map/all_to_all | solution.py:228
  17.6 1.9 %collective-permute-start.1 = (bf16[448,2048]{1,0:T(8,128)(2,1)}, bf16[448,2048]{1,0:T(8,128)(2,1)S(1)}, u32[]{:S(2)}, u32[]{:S(2)}) collective-permute-start(bf16[448,2048]{1,0:T(8,128)(2,1)} %bitcast.37), channel_id=1, source_target_pairs={{0,1},{1,0},{2,3},{3,2},{4,5},{5,4},{6,7},{7,6},{8,9},{9,8},{10,11... | collective-permute-start | bytes 5505032 | tf_op jit(solution)/shard_map/ppermute | solution.py:227
  19.5 2.4 %collective-permute-start = (bf16[448,2048]{1,0:T(8,128)(2,1)}, bf16[448,2048]{1,0:T(8,128)(2,1)}, u32[]{:S(2)}, u32[]{:S(2)}) collective-permute-start(bf16[448,2048]{1,0:T(8,128)(2,1)} %bitcast.29), channel_id=1, source_target_pairs={{0,1},{1,0},{2,3},{3,2},{4,5},{5,4},{6,7},{7,6},{8,9},{9,8},{10,11... | collective-permute-start | bytes 5505032 | tf_op jit(solution)/shard_map/ppermute | solution.py:226
  21.9 1.5 %collective-permute-done.1.later_ref.weight_ref = bf16[448,2048]{1,0:T(8,128)(2,1)S(1)} collective-permute-done((bf16[448,2048]{1,0:T(8,128)(2,1)}, bf16[448,2048]{1,0:T(8,128)(2,1)S(1)}, u32[]{:S(2)}, u32[]{:S(2)}) %collective-permute-start.1) | collective-permute-done | bytes 1835040 | tf_op jit(solution)/shard_map/ppermute | solution.py:227
  23.5 22.3 %all-to-all-done.got_ref = bf16[16,120,128]{2,1,0:T(8,128)(2,1)S(1)} async-done(((bf16[16,120,128]{2,1,0:T(8,128)(2,1)}), bf16[16,120,128]{2,1,0:T(8,128)(2,1)S(1)}, u32[]{:S(2)}, u32[]{:S(2)}) %all-to-all-start) | async-done | bytes 491552 | tf_op jit(solution)/shard_map/all_to_all | solution.py:228
  45.7 0.0 copy-start
  45.7 1.4 %collective-permute-start.2 = (f32[8,2048]{1,0:T(8,128)S(1)}, f32[8,2048]{1,0:T(8,128)S(1)}, u32[]{:S(2)}, u32[]{:S(2)}) collective-permute-start(f32[8,2048]{1,0:T(8,128)S(1)} %join.1), channel_id=1, source_target_pairs={{0,1},{2,3},{4,5},{6,7},{8,9},{10,11},{12,13},{14,15},{16,17},{18,... | collective-permute-start | bytes 196616 | tf_op jit(solution)/shard_map/ppermute | solution.py:240
  47.2 0.0 collective-permute-done.other_hbm
  47.2 0.0 copy-done
  47.2 2.2 %up.1 = f32[512,2048]{1,0:T(8,128)S(1)} custom-call(bf16[16,120,128]{2,1,0:T(8,128)(2,1)S(1)} %all-to-all-done.got_ref, bf16[448,2048]{1,0:T(8,128)(2,1)S(1)} %bitcast.30, bf16[448,2048]{1,0:T(8,128)(2,1)} %collective-permute-done.other_hbm), custom_call_target="tpu_custom_call" | custom-call | tf_op jit(solution)/shard_map/up/pallas_call | solution.py:241
  49.5 0.0 collective-permute-done.2
  49.5 0.5 add_convert_fusion
  50.0 20.8 %all_to_all.15 = f16[4,128,2048]{2,1,0:T(8,128)(2,1)S(1)} all-to-all(f16[4,128,2048]{2,1,0:T(8,128)(2,1)S(1)} %bitcast.34), channel_id=1, replica_groups={{0,128,256,384},{32,160,288,416},{64,192,320,448},{96,224,352,480},{1,3..., dimensions={0} | all-to-all | bytes 4194304 | tf_op jit(solution)/shard_map/all_to_all | solution.py:255
  70.8 0.4 add_convert_fusion.1
  71.2 15.9 %all-gather.2 = f16[4,128,2048]{2,1,0:T(8,128)(2,1)S(1)} all-gather(f16[1,128,2048]{2,1,0:T(8,128)(2,1)S(1)} %add_convert_fusion.1), channel_id=1, replica_groups={{0,32,64,96},{128,160,192,224},{256,288,320,352},{384,416,448,480},{1,1..., dimensions={0}, use_global_device_ids=true | all-gather | bytes 2621440 | tf_op jit(solution)/shard_map/all_gather | solution.py:259
  87.1 0.6 multiply_convert_fusion.3
  87.7 0.0 copy-start.3
  87.7 16.1 %all-gather.3 = f16[512,2048]{1,0:T(8,128)(2,1)S(1)} all-gather(f16[128,2048]{1,0:T(8,128)(2,1)S(1)} %multiply_convert_fusion.3), channel_id=1, replica_groups={{0,128,256,384},{32,160,288,416},{64,192,320,448},{96,224,352,480},{1,3..., dimensions={0}, use_global_device_ids=true | all-gather | bytes 2621440 | tf_op jit(solution)/shard_map/all_gather | solution.py:263
  103.8 0.2 multiply_convert_fusion.active_ref
  104.1 0.0 copy-done.3
  104.1 0.7 fusion.2
  104.8 0.1 copy.9.own_ref
  104.9 0.0 copy-start.1
  104.9 0.0 copy-start.2
  104.9 0.8 down.1
  105.7 25.1 %all_to_all.16.back_ref = bf16[16,112,128]{2,1,0:T(8,128)(2,1)S(1)} all-to-all(bf16[16,112,128]{2,1,0:T(8,128)(2,1)S(1)} %down.1), channel_id=1, replica_groups={{0,2,4,6,8,10,12,14,16,18,20,22,24,26,28,30},{1,3,5,7,9,11,13,15,17,19,..., dimensions={0} | all-to-all | bytes 917504 | tf_op jit(solution)/shard_map/all_to_all | solution.py:276
  130.8 0.0 copy-done.1
  130.8 0.0 copy-done.2
  130.8 1.3 combine.1
  (2 shorter events, 0.0 us)
Async XLA Ops:
  2.4 43.4 %all-to-all-start = ((bf16[16,120,128]{2,1,0:T(8,128)(2,1)}), bf16[16,120,128]{2,1,0:T(8,128)(2,1)S(1)}, u32[]{:S(2)}, u32[]{:S(2)}) async-start(bf16[16,120,128]{2,1,0:T(8,128)(2,1)} %pick.1), calls=%async_computation | async-start | bytes 983040 | tf_op jit(solution)/shard_map/all_to_all | solution.py:228
  17.6 5.9 %collective-permute-start.1 = (bf16[448,2048]{1,0:T(8,128)(2,1)}, bf16[448,2048]{1,0:T(8,128)(2,1)S(1)}, u32[]{:S(2)}, u32[]{:S(2)}) collective-permute-start(bf16[448,2048]{1,0:T(8,128)(2,1)} %bitcast.37), channel_id=1, source_target_pairs={{0,1},{1,0},{2,3},{3,2},{4,5},{5,4},{6,7},{7,6},{8,9},{9,8},{10,11... | collective-permute-start | bytes 5505032 | tf_op jit(solution)/shard_map/ppermute | solution.py:227
  19.5 27.7 %collective-permute-start = (bf16[448,2048]{1,0:T(8,128)(2,1)}, bf16[448,2048]{1,0:T(8,128)(2,1)}, u32[]{:S(2)}, u32[]{:S(2)}) collective-permute-start(bf16[448,2048]{1,0:T(8,128)(2,1)} %bitcast.29), channel_id=1, source_target_pairs={{0,1},{1,0},{2,3},{3,2},{4,5},{5,4},{6,7},{7,6},{8,9},{9,8},{10,11... | collective-permute-start | bytes 5505032 | tf_op jit(solution)/shard_map/ppermute | solution.py:226
  45.7 1.5 %copy-start = (bf16[1,448,2048]{2,1,0:T(8,128)(2,1)S(1)}, bf16[1,448,2048]{2,1,0:T(8,128)(2,1)}, u32[]{:S(2)}) copy-start(bf16[1,448,2048]{2,1,0:T(8,128)(2,1)} %param.10) | copy-start | bytes 5505028
  45.7 3.7 %collective-permute-start.2 = (f32[8,2048]{1,0:T(8,128)S(1)}, f32[8,2048]{1,0:T(8,128)S(1)}, u32[]{:S(2)}, u32[]{:S(2)}) collective-permute-start(f32[8,2048]{1,0:T(8,128)S(1)} %join.1), channel_id=1, source_target_pairs={{0,1},{2,3},{4,5},{6,7},{8,9},{10,11},{12,13},{14,15},{16,17},{18,... | collective-permute-start | bytes 196616 | tf_op jit(solution)/shard_map/ppermute | solution.py:240
  87.7 16.3 %copy-start.3 = (bf16[1,2048,448]{1,2,0:T(8,128)(2,1)S(1)}, bf16[1,2048,448]{1,2,0:T(8,128)(2,1)}, u32[]{:S(2)}) copy-start(bf16[1,2048,448]{1,2,0:T(8,128)(2,1)} %param.11) | copy-start | bytes 5505028
  104.9 25.9 %copy-start.1 = (s32[256,8]{0,1:T(8,128)S(1)}, s32[256,8]{0,1:T(8,128)}, u32[]{:S(2)}) copy-start(s32[256,8]{0,1:T(8,128)} %param.8) | copy-start | bytes 24580
  104.9 25.9 %copy-start.2 = (bf16[256,8]{0,1:T(8,128)(2,1)S(1)}, bf16[256,8]{0,1:T(8,128)(2,1)}, u32[]{:S(2)}) copy-start(bf16[256,8]{0,1:T(8,128)(2,1)} %param.9) | copy-start | bytes 12292

commit v8 on v7

--- a/solution.py
+++ b/solution.py
@@ -139,15 +139,14 @@
             out_ref[i * slots : (i + 1) * slots, j : j + TILE] = term * scale
 
 
-def down_kernel(capacity, own_ref, active_ref, weight_ref, out_ref):
-    width = weight_ref.shape[0]
+def pack_kernel(capacity, own_ref, other_ref, out_ref):
+    width = own_ref.shape[1]
     whole = width // 128
     half = capacity // 2
     rest = width - whole * 128
     chunks = out_ref.shape[0]
-    other = lax.dot_general(active_ref[...], weight_ref[...], NT, preferred_element_type=F32)
     tails = []
-    for i, piece in enumerate((own_ref[...].astype(F32), other)):
+    for i, piece in enumerate((own_ref[...].astype(F32), other_ref[...].astype(F32))):
         for j in range(whole):
             at = (i * whole + j) * capacity
             out_ref[:, at : at + capacity, :] = (
@@ -265,14 +264,15 @@
         (rows.astype(F32) * (1.0 / ACTIVE_GAIN)).astype(BF16) for rows in jnp.split(active, 2)
     )
     own = lax.dot_general(own, down_own, NT, preferred_element_type=F32).astype(BF16)
+    other = lax.dot_general(other, down_other, NT, preferred_element_type=F32).astype(BF16)
     pieces = pl.pallas_call(
-        functools.partial(down_kernel, capacity),
+        functools.partial(pack_kernel, capacity),
         out_shape=jax.ShapeDtypeStruct((chips, 2 * capacity * width // 128, 128), BF16),
-        in_specs=[vmem_spec()] * 3,
+        in_specs=[vmem_spec()] * 2,
         out_specs=vmem_spec(),
         compiler_params=params,
-        name="down",
-    )(own, other, down_other)
+        name="pack",
+    )(own, other)
     back = lax.all_to_all(pieces, "expert", 0, 0, tiled=True, axis_index_groups=rings)
     combined_t = pl.pallas_call(
         functools.partial(combine_kernel, capacity, width),

time: 134 us -> 134 us (level)
  no operation moved by 1% of the time
where the time goes in v8:
time: 134 us; the launch traced here: 132 us
  blocking collectives  77.8 us (58%)
  waiting for transfers between devices  23.8 us (18%)
  starting transfers between devices  21 us (16%)
  Pallas kernels  5.94 us (4%)
  other arithmetic  1.51 us (1%)
  matrix products  1.36 us (1%)
    all_to_all x1, blocking collectives, on_device(): lax.all_to_all(pieces, 'expert', 0, 0, tiled=True, axis_index_groups=rings)  25.1 us
    all_to_all x1, waiting for transfers between devices, on_device(): lax.all_to_all(send, 'expert', 0, 0, tiled=True, axis_index_groups=rings)  22.3 us
    all_to_all x1, blocking collectives, on_device(): lax.all_to_all(terms.reshape(side, side_slots, hidden), plane, 0, 0, tile...  20.8 us
    all_gather x1, blocking collectives, on_device(): lax.all_gather(active, plane, axis=0, tiled=True, axis_index_groups=first)  15.9 us
    all_gather x1, blocking collectives, on_device(): partial = lax.all_gather(partial, plane, axis=0, axis_index_groups=second)  15.9 us
    all_to_all x1, starting transfers between devices, on_device(): lax.all_to_all(send, 'expert', 0, 0, tiled=True, axis_index_groups=rings)  15.2 us
  transfers between devices with their start and end apart: 4, of which 2 were waited for; matrix products, arithmetic and copies ran while one was open for 0% of the time, Pallas kernels for 2%

profile of v8, /device:TPU:6, one launch (start us, length us, event | category | flops | bytes accessed | tf_op | source)
XLA Modules:
  0.0 131.8 jit_solution(13888521549622956231)
XLA Ops:
  0.0 2.3 %pick.1 = bf16[16,120,128]{2,1,0:T(8,128)(2,1)} custom-call(bf16[448,256]{1,0:T(8,128)(2,1)} %bitcast.36, bf16[256]{0:T(256)(128)(2,1)} %scale_hbm.1, s32[8,256]{1,0:T(8,128)} %bitcast.32), custom_call_target="tpu_custom_call" | custom-call | tf_op jit(solution)/shard_map/pick/pallas_call | solution.py:209
  2.4 15.2 %all-to-all-start = ((bf16[16,120,128]{2,1,0:T(8,128)(2,1)}), bf16[16,120,128]{2,1,0:T(8,128)(2,1)S(1)}, u32[]{:S(2)}, u32[]{:S(2)}) async-start(bf16[16,120,128]{2,1,0:T(8,128)(2,1)} %pick.1), calls=%async_computation | async-start | bytes 983040 | tf_op jit(solution)/shard_map/all_to_all | solution.py:227
  17.6 1.9 %collective-permute-start.1 = (bf16[448,2048]{1,0:T(8,128)(2,1)}, bf16[448,2048]{1,0:T(8,128)(2,1)S(1)}, u32[]{:S(2)}, u32[]{:S(2)}) collective-permute-start(bf16[448,2048]{1,0:T(8,128)(2,1)} %bitcast.38), channel_id=1, source_target_pairs={{0,1},{1,0},{2,3},{3,2},{4,5},{5,4},{6,7},{7,6},{8,9},{9,8},{10,11... | collective-permute-start | bytes 5505032 | tf_op jit(solution)/shard_map/ppermute | solution.py:226
  19.5 2.4 %collective-permute-start = (bf16[448,2048]{1,0:T(8,128)(2,1)}, bf16[448,2048]{1,0:T(8,128)(2,1)}, u32[]{:S(2)}, u32[]{:S(2)}) collective-permute-start(bf16[448,2048]{1,0:T(8,128)(2,1)} %bitcast.30), channel_id=1, source_target_pairs={{0,1},{1,0},{2,3},{3,2},{4,5},{5,4},{6,7},{7,6},{8,9},{9,8},{10,11... | collective-permute-start | bytes 5505032 | tf_op jit(solution)/shard_map/ppermute | solution.py:225
  21.9 1.5 %collective-permute-done.1.later_ref = bf16[448,2048]{1,0:T(8,128)(2,1)S(1)} collective-permute-done((bf16[448,2048]{1,0:T(8,128)(2,1)}, bf16[448,2048]{1,0:T(8,128)(2,1)S(1)}, u32[]{:S(2)}, u32[]{:S(2)}) %collective-permute-start.1) | collective-permute-done | bytes 1835040 | tf_op jit(solution)/shard_map/ppermute | solution.py:226
  23.5 22.3 %all-to-all-done.got_ref = bf16[16,120,128]{2,1,0:T(8,128)(2,1)S(1)} async-done(((bf16[16,120,128]{2,1,0:T(8,128)(2,1)}), bf16[16,120,128]{2,1,0:T(8,128)(2,1)S(1)}, u32[]{:S(2)}, u32[]{:S(2)}) %all-to-all-start) | async-done | bytes 491552 | tf_op jit(solution)/shard_map/all_to_all | solution.py:227
  45.7 0.0 copy-start
  45.7 1.4 %collective-permute-start.2 = (f32[8,2048]{1,0:T(8,128)S(1)}, f32[8,2048]{1,0:T(8,128)S(1)}, u32[]{:S(2)}, u32[]{:S(2)}) collective-permute-start(f32[8,2048]{1,0:T(8,128)S(1)} %join.1), channel_id=1, source_target_pairs={{0,1},{2,3},{4,5},{6,7},{8,9},{10,11},{12,13},{14,15},{16,17},{18,... | collective-permute-start | bytes 196616 | tf_op jit(solution)/shard_map/ppermute | solution.py:239
  47.2 0.0 collective-permute-done.other_hbm
  47.2 0.0 copy-done
  47.2 2.2 %up.1 = f32[512,2048]{1,0:T(8,128)S(1)} custom-call(bf16[16,120,128]{2,1,0:T(8,128)(2,1)S(1)} %all-to-all-done.got_ref, bf16[448,2048]{1,0:T(8,128)(2,1)S(1)} %bitcast.31, bf16[448,2048]{1,0:T(8,128)(2,1)} %collective-permute-done.other_hbm), custom_call_target="tpu_custom_call" | custom-call | tf_op jit(solution)/shard_map/up/pallas_call | solution.py:240
  49.5 0.0 collective-permute-done.2
  49.5 0.5 add_convert_fusion
  50.0 20.8 %all_to_all.15 = f16[4,128,2048]{2,1,0:T(8,128)(2,1)S(1)} all-to-all(f16[4,128,2048]{2,1,0:T(8,128)(2,1)S(1)} %bitcast.35), channel_id=1, replica_groups={{0,128,256,384},{32,160,288,416},{64,192,320,448},{96,224,352,480},{1,3..., dimensions={0} | all-to-all | bytes 4194304 | tf_op jit(solution)/shard_map/all_to_all | solution.py:254
  70.8 0.4 add_convert_fusion.1
  71.2 15.9 %all-gather.2 = f16[4,128,2048]{2,1,0:T(8,128)(2,1)S(1)} all-gather(f16[1,128,2048]{2,1,0:T(8,128)(2,1)S(1)} %add_convert_fusion.1), channel_id=1, replica_groups={{0,32,64,96},{128,160,192,224},{256,288,320,352},{384,416,448,480},{1,1..., dimensions={0}, use_global_device_ids=true | all-gather | bytes 2621440 | tf_op jit(solution)/shard_map/all_gather | solution.py:258
  87.1 0.0 copy-start.3
  87.1 0.6 multiply_convert_fusion.4
  87.7 15.9 %all-gather.3 = f16[512,2048]{1,0:T(8,128)(2,1)S(1)} all-gather(f16[128,2048]{1,0:T(8,128)(2,1)S(1)} %multiply_convert_fusion.4), channel_id=1, replica_groups={{0,128,256,384},{32,160,288,416},{64,192,320,448},{96,224,352,480},{1,3..., dimensions={0}, use_global_device_ids=true | all-gather | bytes 2621440 | tf_op jit(solution)/shard_map/all_gather | solution.py:262
  103.7 0.0 copy-done.3
  103.7 0.7 fusion.2
  104.4 0.7 convolution_convert_fusion
  105.0 0.0 copy-start.1
  105.1 0.0 copy-start.2
  105.1 0.1 copy.12.other_ref
  105.2 0.1 copy.11.own_ref
  105.4 0.1 pack.1
  105.5 25.1 %all_to_all.16.back_ref = bf16[16,112,128]{2,1,0:T(8,128)(2,1)S(1)} all-to-all(bf16[16,112,128]{2,1,0:T(8,128)(2,1)S(1)} %pack.1), channel_id=1, replica_groups={{0,2,4,6,8,10,12,14,16,18,20,22,24,26,28,30},{1,3,5,7,9,11,13,15,17,19,..., dimensions={0} | all-to-all | bytes 917504 | tf_op jit(solution)/shard_map/all_to_all | solution.py:276
  130.6 0.0 copy-done.1
  130.6 0.0 copy-done.2
  130.6 1.3 combine.1
  (2 shorter events, 0.0 us)
Async XLA Ops:
  2.4 43.4 %all-to-all-start = ((bf16[16,120,128]{2,1,0:T(8,128)(2,1)}), bf16[16,120,128]{2,1,0:T(8,128)(2,1)S(1)}, u32[]{:S(2)}, u32[]{:S(2)}) async-start(bf16[16,120,128]{2,1,0:T(8,128)(2,1)} %pick.1), calls=%async_computation | async-start | bytes 983040 | tf_op jit(solution)/shard_map/all_to_all | solution.py:227
  17.6 5.9 %collective-permute-start.1 = (bf16[448,2048]{1,0:T(8,128)(2,1)}, bf16[448,2048]{1,0:T(8,128)(2,1)S(1)}, u32[]{:S(2)}, u32[]{:S(2)}) collective-permute-start(bf16[448,2048]{1,0:T(8,128)(2,1)} %bitcast.38), channel_id=1, source_target_pairs={{0,1},{1,0},{2,3},{3,2},{4,5},{5,4},{6,7},{7,6},{8,9},{9,8},{10,11... | collective-permute-start | bytes 5505032 | tf_op jit(solution)/shard_map/ppermute | solution.py:226
  19.5 27.7 %collective-permute-start = (bf16[448,2048]{1,0:T(8,128)(2,1)}, bf16[448,2048]{1,0:T(8,128)(2,1)}, u32[]{:S(2)}, u32[]{:S(2)}) collective-permute-start(bf16[448,2048]{1,0:T(8,128)(2,1)} %bitcast.30), channel_id=1, source_target_pairs={{0,1},{1,0},{2,3},{3,2},{4,5},{5,4},{6,7},{7,6},{8,9},{9,8},{10,11... | collective-permute-start | bytes 5505032 | tf_op jit(solution)/shard_map/ppermute | solution.py:225
  45.7 1.5 %copy-start = (bf16[1,448,2048]{2,1,0:T(8,128)(2,1)S(1)}, bf16[1,448,2048]{2,1,0:T(8,128)(2,1)}, u32[]{:S(2)}) copy-start(bf16[1,448,2048]{2,1,0:T(8,128)(2,1)} %param.10) | copy-start | bytes 5505028
  45.7 3.7 %collective-permute-start.2 = (f32[8,2048]{1,0:T(8,128)S(1)}, f32[8,2048]{1,0:T(8,128)S(1)}, u32[]{:S(2)}, u32[]{:S(2)}) collective-permute-start(f32[8,2048]{1,0:T(8,128)S(1)} %join.1), channel_id=1, source_target_pairs={{0,1},{2,3},{4,5},{6,7},{8,9},{10,11},{12,13},{14,15},{16,17},{18,... | collective-permute-start | bytes 196616 | tf_op jit(solution)/shard_map/ppermute | solution.py:239
  87.1 16.5 %copy-start.3 = (bf16[1,2048,448]{1,2,0:T(8,128)(2,1)S(1)}, bf16[1,2048,448]{1,2,0:T(8,128)(2,1)}, u32[]{:S(2)}) copy-start(bf16[1,2048,448]{1,2,0:T(8,128)(2,1)} %param.11) | copy-start | bytes 5505028
  105.0 25.5 %copy-start.1 = (s32[256,8]{0,1:T(8,128)S(1)}, s32[256,8]{0,1:T(8,128)}, u32[]{:S(2)}) copy-start(s32[256,8]{0,1:T(8,128)} %param.8) | copy-start | bytes 24580
  105.1 25.5 %copy-start.2 = (bf16[256,8]{0,1:T(8,128)(2,1)S(1)}, bf16[256,8]{0,1:T(8,128)(2,1)}, u32[]{:S(2)}) copy-start(bf16[256,8]{0,1:T(8,128)(2,1)} %param.9) | copy-start | bytes 12292
